TPU v7x, 256 devices: a whole 4x4x8 slice. The times are simulated.
256 devices in a mesh: dp: 4 (over y), point: 64 (over z, x, core).
Axes of the slice: x: 4, y: 4, z: 8, core: 2. Of those that a mesh axis runs over, the one named last changes fastest.
Arguments:
- mesh_element_data: bfloat16 [4, 49152, 256], P('dp', 'point'), may hold values from -6 to 6
- loss_sensitivity: bfloat16 [4, 49152, 256], P('dp', 'point'), may hold values from -0.75 to 0.75
- leading_scale_factor: float32 [256], replicated, may hold values from 0.1 to 1.9
- intermediate_map_matrix: bfloat16 [256, 256], replicated, may hold values from -0.375 to 0.375
- partitioned_map_matrix: bfloat16 [256, 256], replicated, may hold values from -0.375 to 0.375
- partition_score_matrix: bfloat16 [32, 64], replicated, may hold values from -1 to 1
- softening_factor: float32 [8], replicated, may hold values from 0.3 to 1
- asking_matrix: bfloat16 [32, 32], replicated, may hold values from -1 to 1
- lookup_matrix: bfloat16 [32, 32], replicated, may hold values from -1 to 1
- content_matrix: bfloat16 [32, 32], replicated, may hold values from -1 to 1
- result_matrix: bfloat16 [256, 256], replicated, may hold values from -0.375 to 0.375
- trailing_scale_factor: float32 [256], replicated, may hold values from 0.1 to 1.9
- expanding_matrix: bfloat16 [256, 1024], replicated, may hold values from -0.375 to 0.375
- contracting_matrix: bfloat16 [1024, 256], replicated, may hold values from -0.1875 to 0.1875
Outputs:
- grad_cells: bfloat16 [4, 49152, 256], P('dp', 'point')
- grad_gain_first: float32 [256], replicated
- grad_proj_mid: float32 [256, 256], replicated
- grad_proj_feat: float32 [256, 256], replicated
- grad_proj_slice: float32 [32, 64], replicated
- grad_temperature: float32 [8], replicated
- grad_w_query: float32 [32, 32], replicated
- grad_w_key: float32 [32, 32], replicated
- grad_w_value: float32 [32, 32], replicated
- grad_w_out: float32 [256, 256], replicated
- grad_gain_second: float32 [256], replicated
- grad_w_up: float32 [256, 1024], replicated
- grad_w_down: float32 [1024, 256], replicated
All inputs are finite; a program needn't handle non-finite values.
Results may differ from a plain program's by a relative error of at most 0.024.
Values sent between devices are 32-bit elements; how exact they have to be, the bound alone decides.
A program may use at most 64 MiB of HBM per device.

v0:
```python
import jax
import jax.numpy as jnp
from jax import lax
from jax.sharding import PartitionSpec as P

D = 256
HEAD_COUNT = 8
SLICES = 64
HEAD_DIM = 32


def norm_rows(values, gain):
    centre = jnp.mean(values, axis=1, keepdims=True)
    centred = values - centre
    spread = jnp.mean(centred * centred, axis=1, keepdims=True)
    return (centred * lax.rsqrt(spread + 1e-05) * gain).astype(jnp.bfloat16)


def partition_share(
    incoming_entries,
    leading_scale_factor,
    intermediate_map_matrix,
    partitioned_map_matrix,
    partition_score_matrix,
    softening_factor,
):
    count = incoming_entries.shape[0]
    normed = norm_rows(incoming_entries, leading_scale_factor)
    middle = jnp.dot(normed, intermediate_map_matrix, preferred_element_type=jnp.float32).reshape(
        count, HEAD_COUNT, HEAD_DIM
    )
    feature = jnp.dot(normed, partitioned_map_matrix, preferred_element_type=jnp.float32).reshape(
        count, HEAD_COUNT, HEAD_DIM
    )
    partition_scores = jnp.einsum(
        "che,em->chm",
        middle,
        partition_score_matrix.astype(jnp.float32),
        precision=lax.Precision.HIGHEST,
    )
    exponentiated_scores = jnp.exp(partition_scores / softening_factor[None, :, None])
    partition_probabilities = exponentiated_scores / jnp.sum(
        exponentiated_scores, axis=2, keepdims=True
    )
    aggregated_states = jnp.einsum(
        "chm,che->hme", partition_probabilities, feature, precision=lax.Precision.HIGHEST
    )
    partition_mass = jnp.sum(partition_probabilities, axis=0)
    return (
        aggregated_states,
        partition_mass,
        partition_probabilities.reshape(count, HEAD_COUNT * SLICES),
    )


def token_mix(aggregated_states, partition_mass, asking_matrix, lookup_matrix, content_matrix):
    tokens = aggregated_states / partition_mass[:, :, None]
    queries = jnp.einsum(
        "hme,ef->hmf", tokens, asking_matrix.astype(jnp.float32), precision=lax.Precision.HIGHEST
    )
    key_rows = jnp.einsum(
        "hme,ef->hmf", tokens, lookup_matrix.astype(jnp.float32), precision=lax.Precision.HIGHEST
    )
    value_rows = jnp.einsum(
        "hme,ef->hmf", tokens, content_matrix.astype(jnp.float32), precision=lax.Precision.HIGHEST
    )
    scores = jnp.einsum(
        "hmf,hnf->hmn", queries, key_rows, precision=lax.Precision.HIGHEST
    ) * HEAD_DIM ** (-0.5)
    exponentiated_scores = jnp.exp(scores)
    probs = exponentiated_scores / jnp.sum(exponentiated_scores, axis=2, keepdims=True)
    return jnp.einsum("hmn,hnf->hmf", probs, value_rows, precision=lax.Precision.HIGHEST)


def mix_part(
    incoming_entries,
    partition_probabilities,
    mixed_tokens,
    result_matrix,
    trailing_scale_factor,
    expanding_matrix,
    contracting_matrix,
):
    count = incoming_entries.shape[0]
    spread = (
        jnp.einsum(
            "chm,hme->che",
            partition_probabilities.reshape(count, HEAD_COUNT, SLICES),
            mixed_tokens,
            precision=lax.Precision.HIGHEST,
        )
        .reshape(count, D)
        .astype(jnp.bfloat16)
    )
    state = incoming_entries + jnp.dot(spread, result_matrix, preferred_element_type=jnp.float32)
    normed = norm_rows(state, trailing_scale_factor)
    hidden = jax.nn.gelu(
        jnp.dot(normed, expanding_matrix, preferred_element_type=jnp.float32), approximate=True
    ).astype(jnp.bfloat16)
    return state + jnp.dot(hidden, contracting_matrix, preferred_element_type=jnp.float32)


def on_device(
    mesh_element_data,
    loss_sensitivity,
    leading_scale_factor,
    intermediate_map_matrix,
    partitioned_map_matrix,
    partition_score_matrix,
    softening_factor,
    asking_matrix,
    lookup_matrix,
    content_matrix,
    result_matrix,
    trailing_scale_factor,
    expanding_matrix,
    contracting_matrix,
):
    incoming_entries = mesh_element_data[0].astype(jnp.float32)
    dyrows = loss_sensitivity[0].astype(jnp.float32)
    firsts, reverse_opening_pass = jax.vjp(
        partition_share,
        incoming_entries,
        leading_scale_factor,
        intermediate_map_matrix,
        partitioned_map_matrix,
        partition_score_matrix,
        softening_factor,
    )
    aggregated_states, partition_mass, partition_probabilities = firsts
    aggregated_states, partition_mass = lax.psum((aggregated_states, partition_mass), "point")
    mixed_tokens, back_mix = jax.vjp(
        token_mix, aggregated_states, partition_mass, asking_matrix, lookup_matrix, content_matrix
    )
    unused_y, back_two = jax.vjp(
        mix_part,
        incoming_entries,
        partition_probabilities,
        mixed_tokens,
        result_matrix,
        trailing_scale_factor,
        expanding_matrix,
        contracting_matrix,
    )
    dx_two, d_weights, d_tokens, g_out, g_gain_two, g_up, g_down = back_two(dyrows)
    d_tokens = lax.psum(d_tokens, "point")
    d_weighted, d_totals, g_query, g_key, g_value = back_mix(d_tokens)
    dx_one, g_gain_one, g_mid, g_feat, g_slice, g_temp = reverse_opening_pass(
        (d_weighted, d_totals, d_weights)
    )
    grad_cells = (dx_one + dx_two).astype(jnp.bfloat16)[None]
    f32 = jnp.float32
    summed = lax.psum(
        (
            g_gain_one,
            g_mid.astype(f32),
            g_feat.astype(f32),
            g_slice.astype(f32),
            g_temp,
            g_out.astype(f32),
            g_gain_two,
            g_up.astype(f32),
            g_down.astype(f32),
        ),
        ("dp", "point"),
    )
    mixed = lax.psum((g_query.astype(f32), g_key.astype(f32), g_value.astype(f32)), "dp")
    derivative_collection = (
        summed[0],
        summed[1],
        summed[2],
        summed[3],
        summed[4],
        mixed[0],
        mixed[1],
        mixed[2],
        summed[5],
        summed[6],
        summed[7],
        summed[8],
    )
    return (
        grad_cells,
        derivative_collection[0],
        derivative_collection[1],
        derivative_collection[2],
        derivative_collection[3],
        derivative_collection[4],
        derivative_collection[5],
        derivative_collection[6],
        derivative_collection[7],
        derivative_collection[8],
        derivative_collection[9],
        derivative_collection[10],
        derivative_collection[11],
    )


def solution(mesh):
    return jax.shard_map(
        on_device,
        mesh=mesh,
        in_specs=(
            P("dp", "point", None),
            P("dp", "point", None),
            P(),
            P(),
            P(),
            P(),
            P(),
            P(),
            P(),
            P(),
            P(),
            P(),
            P(),
            P(),
        ),
        out_specs=(
            P("dp", "point", None),
            P(),
            P(),
            P(),
            P(),
            P(),
            P(),
            P(),
            P(),
            P(),
            P(),
            P(),
            P(),
        ),
        check_vma=False,
    )
```

profile of v0, /device:TPU:1, one launch (start us, length us, event | category | flops | bytes accessed | tf_op | source)
XLA Modules:
  0.0 677.2 jit_solution(338422660913740830)
XLA Ops:
  7.3 1.0 copy.42
  8.3 1.0 copy.44
  9.3 1.2 copy.41
  11.5 2.2 fusion.84
  13.7 2.3 fusion.82
  16.9 128.2 %psum.106 = f32[8,64]{1,0:T(8,128)S(1)} all-reduce(f32[8,64]{1,0:T(8,128)S(1)} %fusion.81), channel_id=1, replica_groups=mesh['dp'=4,'point'=64] {'point'}, use_global_device_ids=true, to_apply=%region_5.0 | all-reduce | flops 512 | bytes 4096 | tf_op jit(solution)/shard_map/psum | solution.py:131
  147.1 46.1 %all-reduce.7.cloned.1.call-done = f32[8,64,32]{1,2,0:T(8,128)} async-done(((f32[8,64,32]{1,2,0:T(8,128)}), f32[8,64,32]{1,2,0:T(8,128)}) %all-reduce.7.cloned.1.call-update) | async-done | bytes 65552 | tf_op jit(solution)/shard_map/psum | solution.py:131
  193.2 1.2 fusion.59
  194.4 1.2 fusion.62
  197.0 1.2 fusion.56
  200.9 2.2 fusion.11
  203.1 2.5 fusion.1
  205.6 1.3 multiply_reduce_fusion.2
  206.9 1.6 fusion.12
  209.5 1.0 fusion.17
  211.6 1.7 fusion.80
  213.3 3.0 fusion.87
  216.6 1.3 multiply_divide_fusion.2
  217.9 169.2 %all-reduce.9.cloned.1.call-done = f32[8,64,32]{1,2,0:T(8,128)} async-done(((f32[8,64,32]{1,2,0:T(8,128)}), f32[8,64,32]{1,2,0:T(8,128)}) %all-reduce.9.cloned.1.call-update) | async-done | bytes 65552 | tf_op jit(solution)/shard_map/psum | solution.py:146
  387.1 1.6 multiply_reduce_fusion.5
  388.8 1.3 fusion.73
  393.7 1.7 multiply_reduce_fusion.1
  397.2 1.0 fusion.19
  398.5 1.0 fusion.18
  399.6 1.3 fusion.34
  403.5 3.1 fusion.27
  406.7 75.8 %all-reduce = (f32[256]{0:T(256)}, f32[32,64]{1,0:T(8,128)}, f32[8]{0:T(128)}, f32[256]{0:T(256)}) all-reduce(f32[256]{0:T(256)S(1)} %get-tuple-element.41, f32[32,64]{1,0:T(8,128)S(1)} %fusion.27, f32[8]{0:T(128)S(1)} %neg.35, f32[256]{0:T(256)S(1)} %copy-done.49), channel_id=1, replica_groups=mesh['dp'=4,'point'=64] {'dp','point'}, use_global_device_ids=true, to_apply=%region_18.0 | all-reduce | flops 2568 | bytes 20544 | tf_op jit(solution)/shard_map/psum | solution.py:153
  483.2 12.6 %all-reduce.2 = (f32[32,32]{1,0:T(8,128)}, f32[32,32]{1,0:T(8,128)}, f32[32,32]{1,0:T(8,128)}) all-reduce(f32[32,32]{1,0:T(8,128)S(1)} %fusion.21, f32[32,32]{1,0:T(8,128)S(1)} %fusion.23, f32[32,32]{1,0:T(8,128)S(1)} %fusion.25), channel_id=1, replica_groups=mesh['dp'=4,'point'=64] {'dp'}, use_global_device_ids=true, to_apply=%region_24.0 | all-reduce | flops 3072 | bytes 24576 | tf_op jit(solution)/shard_map/psum | solution.py:167
  495.8 167.7 %all-reduce.11.cloned.1.call-done = (f32[256,256]{1,0:T(8,128)}, f32[256,256]{1,0:T(8,128)}, f32[256,256]{1,0:T(8,128)}, f32[256,1024]{1,0:T(8,128)}, f32[1024,256]{1,0:T(8,128)}) async-done(((f32[256,256]{1,0:T(8,128)}, f32[256,256]{1,0:T(8,128)}, f32[256,256]{1,0:T(8,128)}, f32[256,1024]{1,0:T(8,128)}, f32[1024,256]{1,0:T(8,128)}), (f32[256,256]{1,0:T(8,128)}, f32[256,256]{1,0:T(8,128)}, ...) | async-done | bytes 2883600 | tf_op jit(solution)/shard_map/psum | solution.py:153
  663.5 1.8 copy.76
  665.3 1.8 copy.77
  667.0 1.7 copy.78
  (166 shorter events, 20.9 us)
Async XLA Ops:
  7.2 192.8 %copy-start = (bf16[256,1024]{1,0:T(8,128)(2,1)S(1)}, bf16[256,1024]{1,0:T(8,128)(2,1)}, u32[]{:S(2)}) copy-start(bf16[256,1024]{1,0:T(8,128)(2,1)} %param.26) | copy-start | bytes 1572868
  7.2 3.6 copy-start.41
  7.2 186.0 %all-reduce.7.cloned.1.call-start = ((), (), s32[]{:S(2)}) async-start(), calls=%async_computation | async-start | bytes 262144 | tf_op jit(solution)/shard_map/psum | solution.py:131
  11.1 2.6 copy-start.9
  11.5 2.2 copy-start.56
  13.7 184.8 %copy-start.16 = (f32[768,8]{0,1:T(8,128)}, f32[768,8]{0,1:T(8,128)S(1)}, u32[]{:S(2)}) copy-start(f32[768,8]{0,1:T(8,128)S(1)} %get-tuple-element.59) | copy-start | bytes 73732
  16.0 130.2 %copy-start.14 = (bf16[1,768,256]{2,1,0:T(8,128)(2,1)S(1)}, bf16[1,768,256]{2,1,0:T(8,128)(2,1)}, u32[]{:S(2)}) copy-start(bf16[1,768,256]{2,1,0:T(8,128)(2,1)} %param.15) | copy-start | bytes 1179652
  16.0 177.3 %copy-start.47 = (bf16[32,32]{1,0:T(8,128)(2,1)S(1)}, bf16[32,32]{1,0:T(8,128)(2,1)}, u32[]{:S(2)}) copy-start(bf16[32,32]{1,0:T(8,128)(2,1)} %param.22) | copy-start | bytes 6148
  16.0 178.4 %copy-start.43 = (bf16[32,32]{1,0:T(8,128)(2,1)S(1)}, bf16[32,32]{1,0:T(8,128)(2,1)}, u32[]{:S(2)}) copy-start(bf16[32,32]{1,0:T(8,128)(2,1)} %param.21) | copy-start | bytes 6148
  16.0 180.9 %copy-start.45 = (bf16[32,32]{1,0:T(8,128)(2,1)S(1)}, bf16[32,32]{1,0:T(8,128)(2,1)}, u32[]{:S(2)}) copy-start(bf16[32,32]{1,0:T(8,128)(2,1)} %param.23) | copy-start | bytes 6148
  16.0 371.1 %all-reduce.9.cloned.1.call-start = ((), (), s32[]{:S(2)}) async-start(), calls=%async_computation.1 | async-start | bytes 262144 | tf_op jit(solution)/shard_map/psum | solution.py:146
  145.1 53.5 %copy-start.34 = (f32[8,64]{1,0:T(8,128)}, f32[8,64]{1,0:T(8,128)S(1)}, u32[]{:S(2)}) copy-start(f32[8,64]{1,0:T(8,128)S(1)} %psum.106) | copy-start | bytes 6148
  194.4 3.7 copy-start.32
  196.9 2.6 copy-start.38
  200.9 2.2 copy-start.51
  209.5 2.1 copy-start.17
  216.3 447.2 %all-reduce.11.cloned.1.call-start = ((), (), s32[]{:S(2)}) async-start(), calls=%async_computation.2 | async-start | bytes 5767168 | tf_op jit(solution)/shard_map/psum | solution.py:153
  387.1 3.0 copy-start.31
  387.1 3.0 copy-start.39
  387.1 3.7 copy-start.23
  388.7 2.6 copy-start.46
  388.7 2.8 copy-start.48
  393.7 4.8 copy-start.15
  397.2 2.3 copy-start.13
  403.5 3.2 copy-start.49
  403.5 78.9 %copy-start.20 = (f32[8,64,32]{1,2,0:T(8,128)S(1)}, f32[8,64,32]{1,2,0:T(8,128)}, u32[]{:S(2)}) copy-start(f32[8,64,32]{1,2,0:T(8,128)} %copy-done.19) | copy-start | bytes 196612
  403.5 78.9 %copy-start.27 = (f32[8,64,32]{1,2,0:T(8,128)S(1)}, f32[8,64,32]{1,2,0:T(8,128)}, u32[]{:S(2)}) copy-start(f32[8,64,32]{1,2,0:T(8,128)} %all-reduce.7.cloned.1.call-done) | copy-start | bytes 196612
  403.5 78.9 %copy-start.36 = (f32[8,64]{1,0:T(8,128)S(1)}, f32[8,64]{1,0:T(8,128)}, u32[]{:S(2)}) copy-start(f32[8,64]{1,0:T(8,128)} %copy-done.34) | copy-start | bytes 6148
  403.5 79.2 %copy-start.29 = (f32[8,64,32]{1,2,0:T(8,128)S(1)}, f32[8,64,32]{1,2,0:T(8,128)}, u32[]{:S(2)}) copy-start(f32[8,64,32]{1,2,0:T(8,128)} %copy-done.28) | copy-start | bytes 196612
  403.5 79.4 %copy-start.25 = (f32[8,64,32]{1,2,0:T(8,128)S(1)}, f32[8,64,32]{1,2,0:T(8,128)}, u32[]{:S(2)}) copy-start(f32[8,64,32]{1,2,0:T(8,128)} %copy-done.24) | copy-start | bytes 196612
  663.5 5.2 copy-start.8
  665.3 4.4 copy-start.7
  (28 other events, 35.4 us)
Sparse Core Ops, SparseCore 0:
  16.1 177.0 all-reduce.6
  216.4 170.5 all-reduce.8
  401.4 262.0 all-reduce.10
where the time goes:
time: 678 us; the launch traced here: 677 us
  waiting for transfers between devices  383 us (56%)
  blocking collectives  217 us (32%)
  matrix products  40.9 us (6%)
  local copies, waits for them, and re-layouts  16.7 us (2%)
  between operations  14.6 us (2%)
    psum x1, waiting for transfers between devices, on_device(): d_tokens = lax.psum(d_tokens, 'point')  169 us
    psum x1, waiting for transfers between devices, on_device(): lax.psum((g_gain_one, g_mid.astype(f32), g_feat.astype(f32), g_slice.asty...  168 us
    psum x1, blocking collectives, on_device(): lax.psum((aggregated_states, partition_mass), 'point')  128 us
    psum x1, blocking collectives, on_device(): lax.psum((g_gain_one, g_mid.astype(f32), g_feat.astype(f32), g_slice.asty...  75.8 us
    psum x1, waiting for transfers between devices, on_device(): lax.psum((aggregated_states, partition_mass), 'point')  46.1 us
    unnamed x124, local copies, waits for them, and re-layouts  16.7 us
  transfers between devices with their start and end apart: 3, of which 3 were waited for; matrix products, arithmetic and copies ran while one was open for 1% of the time, Pallas kernels for 0%

commit v1 on v0

--- a/solution.py
+++ b/solution.py
@@ -1,7 +1,241 @@
+import functools
 import jax
 import jax.numpy as jnp
 from jax import lax
+from jax.experimental import pallas as pl
+from jax.experimental.pallas import tpu as pltpu
 from jax.sharding import PartitionSpec as P
+
+MESH = pl.DeviceIdType.MESH
+f32 = jnp.float32
+
+
+def rcopy(src, dst, ss, rs, dev):
+    return pltpu.make_async_remote_copy(
+        src_ref=src, dst_ref=dst, send_sem=ss, recv_sem=rs, device_id=dev, device_id_type=MESH
+    )
+
+
+def where_am_i():
+    y = lax.axis_index("dp")
+    p = lax.axis_index("point")
+    z = p // 8
+    g = lax.rem(p, 8)
+    x = g // 2
+    c = lax.rem(g, 2)
+    return y, z, x, c, g
+
+
+def barrier(peers):
+    sem = pltpu.get_barrier_semaphore()
+    for dev in peers:
+        pl.semaphore_signal(sem, inc=1, device_id=dev, device_id_type=MESH)
+    pl.semaphore_wait(sem, len(peers))
+
+
+def group_peers(z, g):
+    return [{"point": z * 8 + lax.rem(g + d, 8)} for d in range(1, 8)]
+
+
+def z_peers(z, g):
+    return [{"point": lax.rem(z + d, 8) * 8 + g} for d in range(1, 8)]
+
+
+def x_peers(z, x, c):
+    return [{"point": z * 8 + lax.rem(x + d, 4) * 2 + c} for d in range(1, 4)]
+
+
+def y_peers(y):
+    return [{"dp": lax.rem(y + d, 4)} for d in range(1, 4)]
+
+
+def small_kernel(s_ref, o_ref, rx1, rx2, ss, rs):
+    y, z, x, c, g = where_am_i()
+    gp, zp = group_peers(z, g), z_peers(z, g)
+    barrier(gp + zp)
+    cps = []
+    for d in range(1, 8):
+        cp = rcopy(s_ref.at[lax.rem(g + d, 8)], rx1.at[d - 1], ss.at[0, d - 1], rs.at[0, d - 1], gp[d - 1])
+        cp.start()
+        cps.append(cp)
+    for cp in cps:
+        cp.wait()
+    acc = s_ref[g]
+    for d in range(7):
+        acc = acc + rx1[d]
+    rx2[z] = acc
+    cps = []
+    for d in range(1, 8):
+        cp = rcopy(rx2.at[z], rx2.at[z], ss.at[1, d - 1], rs.at[1, d - 1], zp[d - 1])
+        cp.start()
+        cps.append(cp)
+    for cp in cps:
+        cp.wait()
+    acc = rx2[0]
+    for d in range(1, 8):
+        acc = acc + rx2[d]
+    o_ref[g] = acc
+    cps = []
+    for d in range(1, 8):
+        cp = rcopy(o_ref.at[g], o_ref.at[g], ss.at[2, d - 1], rs.at[2, d - 1], gp[d - 1])
+        cp.start()
+        cps.append(cp)
+    for cp in cps:
+        cp.wait()
+
+
+def small_ar(v, cid):
+    r = v.shape[1]
+    return pl.pallas_call(
+        small_kernel,
+        out_shape=jax.ShapeDtypeStruct((8, r, 128), f32),
+        in_specs=[pl.BlockSpec(memory_space=pltpu.VMEM)],
+        out_specs=pl.BlockSpec(memory_space=pltpu.VMEM),
+        scratch_shapes=[
+            pltpu.VMEM((7, r, 128), f32),
+            pltpu.VMEM((8, r, 128), f32),
+            pltpu.SemaphoreType.DMA((3, 7)),
+            pltpu.SemaphoreType.DMA((3, 7)),
+        ],
+        compiler_params=pltpu.CompilerParams(collective_id=cid, has_side_effects=True),
+    )(v)
+
+
+def add_into(dst, doff, rows, srcs, sl=None):
+    t = min(rows, 64)
+
+    def body(i, _):
+        o = pl.multiple_of(i * t, t)
+        acc = dst[pl.ds(doff + o, t), :]
+        for s in srcs:
+            acc = acc + s[pl.ds(o, t), :]
+        dst[pl.ds(doff + o, t), :] = acc
+        return 0
+
+    lax.fori_loop(0, rows // t, body, 0)
+
+
+def big_kernel(n, g_in, o_ref, gref, rx0, rx1, rx2, rx3, zb, zo, ss, rs):
+    y, z, x, c, g = where_am_i()
+    H, Q, E, F = n // 2, n // 4, n // 16, n // 64
+    K = F // 2
+    core = {"point": z * 8 + x * 2 + (1 - c)}
+    xp, yp, zp = x_peers(z, x, c), y_peers(y), z_peers(z, g)
+    barrier([core] + xp + yp + zp)
+    m8 = lambda v: pl.multiple_of(v, 8)
+    cp = rcopy(g_in.at[pl.ds(m8((1 - c) * H), H)], rx0, ss.at[0], rs.at[0], core)
+    cp.start()
+
+    def cpy(i, _):
+        o = pl.multiple_of(i * 64, 64)
+        gref[pl.ds(o, 64), :] = g_in[pl.ds(m8(c * H) + o, 64), :]
+        return 0
+
+    lax.fori_loop(0, H // 64, cpy, 0)
+    cp.wait()
+    add_into(gref, 0, H, [rx0])
+    cps = []
+    for d in range(1, 4):
+        xi, yi = lax.rem(x + d, 4), lax.rem(y + d, 4)
+        cps.append(rcopy(gref.at[pl.ds(m8(xi * E), E)], rx1.at[0, d - 1], ss.at[d], rs.at[d], xp[d - 1]))
+        cps.append(rcopy(gref.at[pl.ds(m8(Q + yi * E), E)], rx1.at[1, d - 1], ss.at[3 + d], rs.at[3 + d], yp[d - 1]))
+    for cp in cps:
+        cp.start()
+    for cp in cps:
+        cp.wait()
+    a0, b0 = m8(x * E), m8(Q + y * E)
+    add_into(gref, a0, E, [rx1.at[0, d] for d in range(3)])
+    add_into(gref, b0, E, [rx1.at[1, d] for d in range(3)])
+    cps = []
+    for d in range(1, 4):
+        xi, yi = lax.rem(x + d, 4), lax.rem(y + d, 4)
+        cps.append(rcopy(gref.at[pl.ds(m8(a0 + yi * F), F)], rx2.at[0, d - 1], ss.at[6 + d], rs.at[6 + d], yp[d - 1]))
+        cps.append(rcopy(gref.at[pl.ds(m8(b0 + xi * F), F)], rx2.at[1, d - 1], ss.at[9 + d], rs.at[9 + d], xp[d - 1]))
+    for cp in cps:
+        cp.start()
+    for cp in cps:
+        cp.wait()
+    a1, b1 = m8(a0 + y * F), m8(b0 + x * F)
+    acc = gref[pl.ds(a1, F), :]
+    for d in range(3):
+        acc = acc + rx2[0, d]
+    zb[0:F, :] = acc
+    acc = gref[pl.ds(b1, F), :]
+    for d in range(3):
+        acc = acc + rx2[1, d]
+    zb[F : 2 * F, :] = acc
+    def zat(ref, k):
+        return ref.at[pl.ds(m8((k // 2) * K), K), pl.ds(pl.multiple_of(lax.rem(k, 2) * 128, 128), 128)]
+
+    cps = []
+    for d in range(1, 8):
+        zi = lax.rem(z + d, 8)
+        cps.append(rcopy(zat(zb, zi), rx3.at[d - 1], ss.at[12 + d], rs.at[12 + d], zp[d - 1]))
+    for cp in cps:
+        cp.start()
+    for cp in cps:
+        cp.wait()
+    acc = zat(zb, z)[...]
+    for d in range(7):
+        acc = acc + rx3[d]
+    mine = zat(zo, z)
+    mine[...] = acc
+    cps = [rcopy(mine, mine, ss.at[19 + d], rs.at[19 + d], zp[d - 1]) for d in range(1, 8)]
+    for cp in cps:
+        cp.start()
+    for cp in cps:
+        cp.wait()
+    h0 = m8(c * H)
+    o_ref[pl.ds(h0 + a1, F), :] = zo[0:F, :]
+    o_ref[pl.ds(h0 + b1, F), :] = zo[F : 2 * F, :]
+    cps = []
+    ra, rb = o_ref.at[pl.ds(h0 + a1, F)], o_ref.at[pl.ds(h0 + b1, F)]
+    for d in range(1, 4):
+        cps.append(rcopy(ra, ra, ss.at[26 + d], rs.at[26 + d], yp[d - 1]))
+        cps.append(rcopy(rb, rb, ss.at[29 + d], rs.at[29 + d], xp[d - 1]))
+    for cp in cps:
+        cp.start()
+    for cp in cps:
+        cp.wait()
+    cps = []
+    ra, rb = o_ref.at[pl.ds(h0 + a0, E)], o_ref.at[pl.ds(h0 + b0, E)]
+    for d in range(1, 4):
+        cps.append(rcopy(ra, ra, ss.at[32 + d], rs.at[32 + d], xp[d - 1]))
+        cps.append(rcopy(rb, rb, ss.at[35 + d], rs.at[35 + d], yp[d - 1]))
+    for cp in cps:
+        cp.start()
+    for cp in cps:
+        cp.wait()
+    half = o_ref.at[pl.ds(h0, H)]
+    cp = rcopy(half, half, ss.at[39], rs.at[39], core)
+    cp.start()
+    cp.wait()
+
+
+def big_ar(v, cid):
+    n = v.shape[0]
+    H, E, F = n // 2, n // 16, n // 64
+    return pl.pallas_call(
+        functools.partial(big_kernel, n),
+        out_shape=jax.ShapeDtypeStruct((n, 256), f32),
+        in_specs=[pl.BlockSpec(memory_space=pltpu.VMEM)],
+        out_specs=pl.BlockSpec(memory_space=pltpu.VMEM),
+        scratch_shapes=[
+            pltpu.VMEM((H, 256), f32),
+            pltpu.VMEM((H, 256), f32),
+            pltpu.VMEM((2, 3, E, 256), f32),
+            pltpu.VMEM((2, 3, F, 256), f32),
+            pltpu.VMEM((7, F // 2, 128), f32),
+            pltpu.VMEM((2 * F, 256), f32),
+            pltpu.VMEM((2 * F, 256), f32),
+            pltpu.SemaphoreType.DMA((40,)),
+            pltpu.SemaphoreType.DMA((40,)),
+        ],
+        compiler_params=pltpu.CompilerParams(
+            collective_id=cid, has_side_effects=True, vmem_limit_bytes=40 * 2**20
+        ),
+    )(v)
+
 
 D = 256
 HEAD_COUNT = 8
@@ -128,7 +362,13 @@
         softening_factor,
     )
     aggregated_states, partition_mass, partition_probabilities = firsts
-    aggregated_states, partition_mass = lax.psum((aggregated_states, partition_mass), "point")
+    rows = jnp.concatenate(
+        [aggregated_states.reshape(8, 16, 128), jnp.pad(partition_mass.reshape(8, 1, 64), ((0, 0), (0, 7), (0, 64)))],
+        axis=1,
+    )
+    rows = small_ar(rows, 0)
+    aggregated_states = rows[:, :16].reshape(HEAD_COUNT, SLICES, HEAD_DIM)
+    partition_mass = rows[:, 16, :64]
     mixed_tokens, back_mix = jax.vjp(
         token_mix, aggregated_states, partition_mass, asking_matrix, lookup_matrix, content_matrix
     )
@@ -143,28 +383,38 @@
         contracting_matrix,
     )
     dx_two, d_weights, d_tokens, g_out, g_gain_two, g_up, g_down = back_two(dyrows)
-    d_tokens = lax.psum(d_tokens, "point")
+    d_tokens = small_ar(d_tokens.reshape(8, 16, 128), 1).reshape(HEAD_COUNT, SLICES, HEAD_DIM)
     d_weighted, d_totals, g_query, g_key, g_value = back_mix(d_tokens)
     dx_one, g_gain_one, g_mid, g_feat, g_slice, g_temp = reverse_opening_pass(
         (d_weighted, d_totals, d_weights)
     )
     grad_cells = (dx_one + dx_two).astype(jnp.bfloat16)[None]
     f32 = jnp.float32
-    summed = lax.psum(
-        (
-            g_gain_one,
-            g_mid.astype(f32),
-            g_feat.astype(f32),
-            g_slice.astype(f32),
-            g_temp,
-            g_out.astype(f32),
-            g_gain_two,
-            g_up.astype(f32),
-            g_down.astype(f32),
-        ),
-        ("dp", "point"),
-    )
-    mixed = lax.psum((g_query.astype(f32), g_key.astype(f32), g_value.astype(f32)), "dp")
+    first = (lax.axis_index("point") == 0).astype(f32)
+    smalls = (g_gain_one, g_slice.astype(f32), g_temp, g_gain_two) + tuple(
+        t.astype(f32) * first for t in (g_query, g_key, g_value)
+    )
+    sizes = [t.size for t in smalls]
+    flat = jnp.concatenate([t.reshape(-1) for t in smalls])
+    flat = jnp.pad(flat, (0, 256 * 256 - flat.size)).reshape(256, 256)
+    up = g_up.astype(f32)
+    stack = jnp.concatenate(
+        [g_down.astype(f32)]
+        + [up[:, k * 256 : (k + 1) * 256] for k in range(4)]
+        + [g_out.astype(f32), g_mid.astype(f32), g_feat.astype(f32), flat]
+    )
+    stack = big_ar(stack, 2)
+    flat = stack[2816:].reshape(-1)
+    parts, at = [], 0
+    for t, size in zip(smalls, sizes):
+        parts.append(flat[at : at + size].reshape(t.shape))
+        at += size
+    up = jnp.concatenate([stack[1024 + k * 256 : 1280 + k * 256] for k in range(4)], axis=1)
+    summed = (
+        parts[0], stack[2304:2560], stack[2560:2816], parts[1], parts[2],
+        stack[2048:2304], parts[3], up, stack[:1024],
+    )
+    mixed = parts[4:]
     derivative_collection = (
         summed[0],
         summed[1],

time: 678 us -> 176 us (0.26)
  waiting for transfers between devices: 383 us -> 0 us
  blocking collectives: 217 us -> 0 us
  Pallas kernels: 0 us -> 95.2 us
  between operations: 14.6 us -> 1.79 us
  local copies, waits for them, and re-layouts: 16.7 us -> 27.5 us
    psum x3 -> x0, waiting for transfers between devices: 383 us -> none  [the longest x1 169 us: on_device(): d_tokens = lax.psum(d_tokens, 'point')]
    psum x3 -> x0, blocking collectives: 217 us -> none  [the longest x1 128 us: on_device(): lax.psum((aggregated_states, partition_mass), 'point')]
    pallas_call x0 -> x3, Pallas kernels: none -> 95.2 us  [the longest x1 54.5 us: big_ar(): pl.pallas_call(functools.partial(big_kernel, n), out_shape=jax.ShapeDtype...]
    slice x0 -> x9, local copies, waits for them, and re-layouts: none -> 8.25 us  [the longest x5 3.2 us: on_device(): parts.append(flat[at:at + size].reshape(t.shape))]
    reshape x0 -> x14, local copies, waits for them, and re-layouts: none -> 7.71 us  [the longest x4 2.9 us: on_device(): flat = jnp.concatenate([t.reshape(-1) for t in smalls])]
    unnamed x124 -> x142, local copies, waits for them, and re-layouts: 16.7 us -> 11.4 us
  transfers between devices with their start and end apart: 3 -> 0, of which waited for: 3 -> 0; matrix products, arithmetic and copies ran while one was open for 1% -> 0% of each run, Pallas kernels for 0% -> 0%
where the time goes in v1:
time: 176 us; the launch traced here: 175 us
  Pallas kernels  95.2 us (54%)
  matrix products  43.9 us (25%)
  local copies, waits for them, and re-layouts  27.5 us (16%)
  other arithmetic  6.64 us (4%)
  between operations  1.79 us (1%)
    pallas_call x1, Pallas kernels, big_ar(): pl.pallas_call(functools.partial(big_kernel, n), out_shape=jax.ShapeDtype...  54.5 us
    pallas_call x2, Pallas kernels, small_ar(): pl.pallas_call(small_kernel, out_shape=jax.ShapeDtypeStruct((8, r, 128),...  40.6 us
    unnamed x142, local copies, waits for them, and re-layouts  11.4 us
    dot_general x3, matrix products, partition_share(): jnp.einsum('chm,che->hme', partition_probabilities, feature, precision=la...  5.07 us
    dot_general x2, matrix products, mix_part(): jnp.dot(hidden, contracting_matrix, preferred_element_type=jnp.float32)  4.94 us
    dot_general x3, matrix products, partition_share(): jnp.einsum('che,em->chm', middle, partition_score_matrix.astype(jnp.float...  4.63 us
    dot_general x3, matrix products, token_mix(): jnp.einsum('hmf,hnf->hmn', queries, key_rows, precision=lax.Precision.HIG...  4.36 us
    dot_general x3, matrix products, mix_part(): jnp.dot(normed, expanding_matrix, preferred_element_type=jnp.float32)  4.2 us

profile of v1, /device:TPU:1, one launch (start us, length us, event | category | flops | bytes accessed | tf_op | source)
XLA Modules:
  0.0 175.0 jit_solution(3943320622123889101)
XLA Ops:
  0.7 1.2 copy.47
  4.3 2.2 %fusion.91 = (f32[768,8]{0,1:T(8,128)S(1)}, f32[768,8,64]{0,2,1:T(8,128)S(1)}, f32[768,8,64]{0,2,1:T(8,128)}) fusion(f32[8]{0:T(128)S(1)} %copy-done.62, f32[768,8,32]{0,2,1:T(8,128)S(1)} %fusion.52, bf16[32,64]{1,0:T(8,128)(2,1)S(1)} %copy-done.60), kind=kOutput, calls=%fused_computation.155 | convolution fusion | flops 151775232 | bytes 3960864 | tf_op jit(solution)/shard_map/jvp(che,em->chm)/dot_general | solution.py:269
  7.8 1.6 fusion.89
  10.4 22.9 %shard_map.237 = f32[8,24,128]{2,1,0:T(8,128)} custom-call(f32[8,24,128]{2,1,0:T(8,128)} %select_maximum_fusion.s_ref), custom_call_target="tpu_custom_call" | custom-call | tf_op jit(solution)/shard_map/pallas_call | solution.py:89
  40.0 2.7 %fusion.1 = bf16[768,1024]{1,0:T(8,128)(2,1)S(1)} fusion(f32[768,1024]{1,0:T(8,128)S(1)} %fusion.82, bf16[1024,256]{1,0:T(8,128)(2,1)S(1)} %copy-done.59, bf16[1,768,256]{2,1,0:T(8,128)(2,1)S(1)} %copy-done.22), kind=kOutput, calls=%fused_computation.5 | convolution fusion | flops 419954688 | bytes 5636096 | tf_op jit(solution)/shard_map/transpose(jvp())/dot_general | solution.py:334
  42.6 1.3 multiply_reduce_fusion.2
  44.0 1.1 fusion.90
  45.1 1.9 %copy.56 = bf16[1,768,256]{1,2,0:T(8,128)(2,1)} copy(bf16[1,768,256]{2,1,0:T(8,128)(2,1)} %param.15) | data formatting | bytes 786432 | tf_op args[1]
  47.0 1.5 convolution_convert_fusion.5
  49.3 1.6 fusion.87
  51.7 17.7 %shard_map.238 = f32[8,16,128]{2,1,0:T(8,128)} custom-call(f32[8,16,128]{2,1,0:T(8,128)} %reshape.278.s_ref), custom_call_target="tpu_custom_call" | custom-call | tf_op jit(solution)/shard_map/pallas_call | solution.py:89
  71.0 1.7 multiply_reduce_fusion.5
  73.4 2.1 %fusion.80 = f32[8,64,32]{1,2,0:T(8,128)} fusion(f32[8,64,32]{1,2,0:T(8,128)} %copy-done.34, f32[8,64,64]{1,2,0:T(8,128)} %copy-done.12, f32[8,64,64]{1,2,0:T(8,128)S(1)} %get-tuple-element.67, f32[8,64]{1,0:T(8,128)S(1)} %neg.31, f32[8,64]{1,0:T(8,128)} %copy-done.45), kind=kOutput, calls=%fused_computation.148 | convolution fusion | flops 12713984 | bytes 397312 | tf_op jit(solution)/shard_map/transpose(jvp(hmf,hnf->hmn))/dot_general | solution.py:301
  75.5 1.8 %fusion.26 = f32[32,32]{1,0:T(8,128)} fusion(f32[8,64,32]{1,2,0:T(8,128)} %fusion.80, f32[]{:T(128)S(6)} %convert_element_type.160, f32[8,64,32]{1,2,0:T(8,128)} %copy-done.16, f32[8,64]{1,0:T(8,128)} %bitcast.192), kind=kOutput, calls=%fused_computation.59 | convolution fusion | flops 6310912 | bytes 137220 | tf_op jit(solution)/shard_map/transpose(jvp(hme,ef->hmf))/dot_general | solution.py:292
  77.3 1.4 reshape.284
  78.7 1.7 fusion.81
  81.0 1.8 %fusion.29 = f32[32,32]{1,0:T(8,128)} fusion(f32[8,64,32]{1,2,0:T(8,128)S(1)} %fusion.81, f32[]{:T(128)S(6)} %convert_element_type.160, f32[8,64,32]{1,2,0:T(8,128)} %copy-done.16, f32[8,64]{1,0:T(8,128)} %bitcast.193), kind=kOutput, calls=%fused_computation.62 | convolution fusion | flops 6310912 | bytes 137220 | tf_op jit(solution)/shard_map/transpose(jvp(hme,ef->hmf))/dot_general | solution.py:295
  82.8 1.4 reshape.285
  84.2 1.5 fusion.58
  86.4 1.2 fusion.32
  88.7 1.1 convolution_add_fusion.2
  90.5 1.3 multiply_reduce_fusion.6
  91.8 1.8 %fusion.60 = bf16[8,32,768]{2,1,0:T(8,128)(2,1)S(1)} fusion(f32[8,64,32]{1,2,0:T(8,128)S(1)} %get-tuple-element.69, f32[8,64]{1,0:T(8,128)} %bitcast.196, f32[768,8,64]{0,2,1:T(8,128)S(1)} %get-tuple-element.48, f32[768,8]{0,1:T(8,128)} %copy-done.26), kind=kOutput, calls=%fused_computation.115 | convolution fusion | flops 151404544 | bytes 2058240 | tf_op jit(solution)/shard_map/transpose(jvp(chm,che->hme))/dot_general | solution.py:279
  94.6 1.7 multiply_reduce_fusion.1
  100.2 1.6 fusion.34
  102.2 2.2 %fusion.13 = f32[256,1024]{1,0:T(8,128)S(1)} fusion(bf16[768,1024]{1,0:T(8,128)(2,1)} %copy-done.6, f32[768,256]{0,1:T(8,128)S(1)} %get-tuple-element.64, f32[256]{0:T(256)S(1)} %copy-done.49, f32[768]{0:T(1024)S(1)} %fusion.75, f32[768]{0:T(1024)S(1)} %broadcast_multiply_fusion), kind=kOutput, calls=%fused_computation.25 | convolution fusion | flops 403701760 | bytes 3415040 | tf_op jit(solution)/shard_map/transpose(jvp())/dot_general | solution.py:332
  104.6 2.3 %fusion.12 = f32[3072,256]{1,0:T(8,128)S(1)} fusion(f32[768,1024]{1,0:T(8,128)S(1)} %copy-done.5, bf16[1,768,256]{2,1,0:T(8,128)(2,1)} %param.15), kind=kOutput, calls=%fused_computation.23 | convolution fusion | flops 410255360 | bytes 4587520 | tf_op jit(solution)/shard_map/transpose(jvp())/dot_general | solution.py:334
  108.6 54.5 %shard_map.239 = f32[3072,256]{1,0:T(8,128)S(1)} custom-call(f32[3072,256]{1,0:T(8,128)S(1)} %constant_dynamic-update-slice_fusion.g_in), custom_call_target="tpu_custom_call" | custom-call | tf_op jit(solution)/shard_map/pallas_call | solution.py:218
  163.1 1.2 fusion.92
  164.3 1.1 pad_maximum_fusion
  168.8 2.3 %slice.94 = f32[1024,256]{1,0:T(8,128)} slice(f32[3072,256]{1,0:T(8,128)} %copy-done.1), slice={[0:1024], [0:256]} | slice | bytes 2097152 | tf_op jit(solution)/shard_map/slice | solution.py:415
  172.5 1.3 slice.78
  (203 shorter events, 30.7 us)
Async XLA Ops:
  0.6 38.6 %copy-start = (bf16[256,1024]{1,0:T(8,128)(2,1)S(1)}, bf16[256,1024]{1,0:T(8,128)(2,1)}, u32[]{:S(2)}) copy-start(bf16[256,1024]{1,0:T(8,128)(2,1)} %param.26) | copy-start | bytes 1572868
  0.7 3.6 %copy-start.60 = (bf16[32,64]{1,0:T(8,128)(2,1)S(1)}, bf16[32,64]{1,0:T(8,128)(2,1)}, u32[]{:S(2)}) copy-start(bf16[32,64]{1,0:T(8,128)(2,1)} %param.19) | copy-start | bytes 12292
  0.7 3.5 %copy-start.62 = (f32[8]{0:T(128)S(1)}, f32[8]{0:T(128)}, u32[]{:S(2)}) copy-start(f32[8]{0:T(128)} %param.20) | copy-start | bytes 100
  2.1 4.3 %copy-start.40 = (f32[768]{0:T(1024)}, f32[768]{0:T(1024)S(1)}, u32[]{:S(2)}) copy-start(f32[768]{0:T(1024)S(1)} %fusion.40) | copy-start | bytes 9220
  2.1 4.4 %copy-start.37 = (f32[768]{0:T(1024)}, f32[768]{0:T(1024)S(1)}, u32[]{:S(2)}) copy-start(f32[768]{0:T(1024)S(1)} %fusion.74) | copy-start | bytes 9220
  4.3 2.3 %copy-start.50 = (f32[256]{0:T(256)S(1)}, f32[256]{0:T(256)}, u32[]{:S(2)}) copy-start(f32[256]{0:T(256)} %param.16) | copy-start | bytes 3076
  6.5 31.0 %copy-start.26 = (f32[768,8]{0,1:T(8,128)}, f32[768,8]{0,1:T(8,128)S(1)}, u32[]{:S(2)}) copy-start(f32[768,8]{0,1:T(8,128)S(1)} %get-tuple-element.47) | copy-start | bytes 73732
  7.8 27.4 %copy-start.56 = (bf16[32,32]{1,0:T(8,128)(2,1)S(1)}, bf16[32,32]{1,0:T(8,128)(2,1)}, u32[]{:S(2)}) copy-start(bf16[32,32]{1,0:T(8,128)(2,1)} %param.22) | copy-start | bytes 6148
  9.4 26.1 %copy-start.54 = (bf16[32,32]{1,0:T(8,128)(2,1)S(1)}, bf16[32,32]{1,0:T(8,128)(2,1)}, u32[]{:S(2)}) copy-start(bf16[32,32]{1,0:T(8,128)(2,1)} %param.21) | copy-start | bytes 6148
  9.4 27.0 %copy-start.55 = (bf16[32,32]{1,0:T(8,128)(2,1)S(1)}, bf16[32,32]{1,0:T(8,128)(2,1)}, u32[]{:S(2)}) copy-start(bf16[32,32]{1,0:T(8,128)(2,1)} %param.23) | copy-start | bytes 6148
  34.4 4.0 %copy-start.16 = (f32[8,64,32]{1,2,0:T(8,128)}, f32[8,64,32]{1,2,0:T(8,128)S(1)}, u32[]{:S(2)}) copy-start(f32[8,64,32]{1,2,0:T(8,128)S(1)} %copy.53) | copy-start | bytes 196612
  40.0 2.7 %copy-start.4 = (f32[768,1024]{1,0:T(8,128)}, f32[768,1024]{1,0:T(8,128)S(1)}, u32[]{:S(2)}) copy-start(f32[768,1024]{1,0:T(8,128)S(1)} %fusion.82) | copy-start | bytes 9437188
  42.6 2.5 %copy-start.6 = (bf16[768,1024]{1,0:T(8,128)(2,1)}, bf16[768,1024]{1,0:T(8,128)(2,1)S(1)}, u32[]{:S(2)}) copy-start(bf16[768,1024]{1,0:T(8,128)(2,1)S(1)} %fusion.1) | copy-start | bytes 4718596
  72.7 2.7 %copy-start.57 = (f32[8,64]{1,0:T(8,128)}, f32[8,64]{1,0:T(8,128)S(1)}, u32[]{:S(2)}) copy-start(f32[8,64]{1,0:T(8,128)S(1)} %neg.31) | copy-start | bytes 6148
  90.5 3.1 %copy-start.11 = (bf16[768,256]{0,1:T(8,128)(2,1)S(1)}, bf16[768,256]{0,1:T(8,128)(2,1)}, u32[]{:S(2)}) copy-start(bf16[768,256]{0,1:T(8,128)(2,1)} %copy-done.10) | copy-start | bytes 1179652
  90.5 3.1 %copy-start.29 = (f32[8,64,32]{1,2,0:T(8,128)S(1)}, f32[8,64,32]{1,2,0:T(8,128)}, u32[]{:S(2)}) copy-start(f32[8,64,32]{1,2,0:T(8,128)} %copy-done.28) | copy-start | bytes 196612
  91.8 2.7 %copy-start.27 = (f32[768,8]{0,1:T(8,128)S(1)}, f32[768,8]{0,1:T(8,128)}, u32[]{:S(2)}) copy-start(f32[768,8]{0,1:T(8,128)} %copy-done.26) | copy-start | bytes 73732
  91.8 2.7 %copy-start.14 = (f32[768,8,32]{0,2,1:T(8,128)S(1)}, f32[768,8,32]{0,2,1:T(8,128)}, u32[]{:S(2)}) copy-start(f32[768,8,32]{0,2,1:T(8,128)} %copy-done.13) | copy-start | bytes 2359300
  91.8 2.7 %copy-start.43 = (f32[8,1,64]{2,1,0:T(1,128)S(1)}, f32[8,1,64]{2,1,0:T(1,128)}, u32[]{:S(2)}) copy-start(f32[8,1,64]{2,1,0:T(1,128)} %copy-done.42) | copy-start | bytes 6148
  93.6 5.3 %copy-start.23 = (bf16[8,32,768]{2,1,0:T(8,128)(2,1)}, bf16[8,32,768]{2,1,0:T(8,128)(2,1)S(1)}, u32[]{:S(2)}) copy-start(bf16[8,32,768]{2,1,0:T(8,128)(2,1)S(1)} %fusion.60) | copy-start | bytes 1179652
  97.9 2.4 %copy-start.65 = (f32[768,8,32]{0,2,1:T(8,128)S(1)}, f32[768,8,32]{0,2,1:T(8,128)}, u32[]{:S(2)}) copy-start(f32[768,8,32]{0,2,1:T(8,128)} %copy-done.64) | copy-start | bytes 2359300
  99.3 2.6 %copy-start.35 = (f32[768]{0:T(1024)}, f32[768]{0:T(1024)S(1)}, u32[]{:S(2)}) copy-start(f32[768]{0:T(1024)S(1)} %multiply_multiply_fusion.3) | copy-start | bytes 9220
  99.3 2.7 %copy-start.46 = (f32[1024]{0:T(1024)S(1)}, f32[1024]{0:T(1024)}, u32[]{:S(2)}) copy-start(f32[1024]{0:T(1024)} %reshape.284) | copy-start | bytes 12292
  99.3 2.7 %copy-start.47 = (f32[1024]{0:T(1024)S(1)}, f32[1024]{0:T(1024)}, u32[]{:S(2)}) copy-start(f32[1024]{0:T(1024)} %reshape.285) | copy-start | bytes 12292
  99.3 2.7 %copy-start.58 = (f32[256]{0:T(256)S(1)}, f32[256]{0:T(256)}, u32[]{:S(2)}) copy-start(f32[256]{0:T(256)} %get-tuple-element.39) | copy-start | bytes 3076
  102.2 2.4 %copy-start.5 = (f32[768,1024]{1,0:T(8,128)S(1)}, f32[768,1024]{1,0:T(8,128)}, u32[]{:S(2)}) copy-start(f32[768,1024]{1,0:T(8,128)} %copy-done.4) | copy-start | bytes 9437188
  104.6 2.5 %copy-start.2 = (f32[768,256]{0,1:T(8,128)S(1)}, f32[768,256]{0,1:T(8,128)}, u32[]{:S(2)}) copy-start(f32[768,256]{0,1:T(8,128)} %get-tuple-element.46) | copy-start | bytes 2359300
  104.6 2.5 %copy-start.3 = (bf16[1,768,256]{1,2,0:T(8,128)(2,1)S(1)}, bf16[1,768,256]{1,2,0:T(8,128)(2,1)}, u32[]{:S(2)}) copy-start(bf16[1,768,256]{1,2,0:T(8,128)(2,1)} %copy.56) | copy-start | bytes 1179652
  104.6 2.5 %copy-start.9 = (bf16[8,32,768]{2,1,0:T(8,128)(2,1)S(1)}, bf16[8,32,768]{2,1,0:T(8,128)(2,1)}, u32[]{:S(2)}) copy-start(bf16[8,32,768]{2,1,0:T(8,128)(2,1)} %copy-done.8) | copy-start | bytes 1179652
  164.3 9.4 %copy-start.44 = (f32[768]{0:T(1024)S(1)}, f32[768]{0:T(1024)}, u32[]{:S(2)}) copy-start(f32[768]{0:T(1024)} %get-tuple-element.42) | copy-start | bytes 9220
  164.3 9.4 %copy-start.36 = (f32[768]{0:T(1024)S(1)}, f32[768]{0:T(1024)}, u32[]{:S(2)}) copy-start(f32[768]{0:T(1024)} %copy-done.35) | copy-start | bytes 9220
  164.3 9.4 %copy-start.53 = (f32[256]{0:T(256)S(1)}, f32[256]{0:T(256)}, u32[]{:S(2)}) copy-start(f32[256]{0:T(256)} %param.16) | copy-start | bytes 3076
  (34 other events, 47.2 us)

commit v2 on v0

v2 whole, which is shorter than its diff:
```python
import functools
import jax
import jax.numpy as jnp
from jax import lax
from jax.experimental import pallas as pl
from jax.experimental.pallas import tpu as pltpu
from jax.sharding import PartitionSpec as P

MESH = pl.DeviceIdType.MESH
HIGHEST = lax.Precision.HIGHEST
f32 = jnp.float32
bf16 = jnp.bfloat16

CELLS = 768
D = 256
FF = 1024
HEADS = 8
SLICES = 64
HEAD_DIM = 32
HM = HEADS * SLICES
TILE = 256
EPS = 1e-05
N1 = 2048
N2 = 1024
SMALL = 768
GELU_C = 0.7978845608028654
GELU_A = 0.044715


def rcopy(src, dst, ss, rs, dev):
    return pltpu.make_async_remote_copy(
        src_ref=src, dst_ref=dst, send_sem=ss, recv_sem=rs, device_id=dev, device_id_type=MESH
    )


def m8(v):
    return pl.multiple_of(v, 8)


class Place:
    def __init__(self):
        self.y = lax.axis_index("dp")
        p = lax.axis_index("point")
        self.z = p // 8
        self.g = lax.rem(p, 8)
        self.x = self.g // 2
        self.c = lax.rem(self.g, 2)
        z, x, c, g, y = self.z, self.x, self.c, self.g, self.y
        self.core = {"point": z * 8 + x * 2 + (1 - c)}
        self.gp = [{"point": z * 8 + lax.rem(g + d, 8)} for d in range(1, 8)]
        self.zp = [{"point": lax.rem(z + d, 8) * 8 + g} for d in range(1, 8)]
        self.xp = [{"point": z * 8 + lax.rem(x + d, 4) * 2 + c} for d in range(1, 4)]
        self.yp = [{"dp": lax.rem(y + d, 4)} for d in range(1, 4)]


class SmallSum:
    def __init__(self, at, s, o, rx1, rx2, ss, rs):
        self.at, self.s, self.o, self.rx1, self.rx2, self.ss, self.rs = at, s, o, rx1, rx2, ss, rs
        self.stage = 0
        self.copies = []

    def wait(self):
        for cp in self.copies:
            cp.wait()
        self.copies = []

    def step(self):
        at, s, o, rx1, rx2, ss, rs = self.at, self.s, self.o, self.rx1, self.rx2, self.ss, self.rs
        self.wait()
        k = self.stage
        self.stage += 1
        if k == 0:
            for d in range(1, 8):
                src = s.at[lax.rem(at.g + d, 8)]
                self.copies.append(rcopy(src, rx1.at[d - 1], ss.at[0, d - 1], rs.at[0, d - 1], at.gp[d - 1]))
        elif k == 1:
            acc = s[at.g]
            for d in range(7):
                acc = acc + rx1[d]
            rx2[at.z] = acc
            mine = rx2.at[at.z]
            for d in range(1, 8):
                self.copies.append(rcopy(mine, mine, ss.at[1, d - 1], rs.at[1, d - 1], at.zp[d - 1]))
        elif k == 2:
            acc = rx2[0]
            for d in range(1, 8):
                acc = acc + rx2[d]
            o[at.g] = acc
            mine = o.at[at.g]
            for d in range(1, 8):
                self.copies.append(rcopy(mine, mine, ss.at[2, d - 1], rs.at[2, d - 1], at.gp[d - 1]))
        for cp in self.copies:
            cp.start()


def add_rows(dst, d0, base, b0, srcs, rows):
    t = min(rows, 64)

    def body(i, _):
        o = pl.multiple_of(i * t, t)
        acc = base[pl.ds(m8(b0 + o), t), :]
        for s in srcs:
            acc = acc + s[pl.ds(o, t), :]
        dst[pl.ds(m8(d0 + o), t), :] = acc
        return 0

    lax.fori_loop(0, rows // t, body, 0)


class BigSum:
    def __init__(self, n, at, src, o, bufs, ss, rs):
        self.n, self.at, self.src, self.o, self.ss, self.rs = n, at, src, o, ss, rs
        self.gref, self.rx0, self.rx1, self.rx2, self.rx3, self.zb, self.zo = bufs
        self.H, self.Q, self.E, self.F = n // 2, n // 4, n // 16, n // 64
        self.K = self.F // 2
        E, F, Q, H = self.E, self.F, self.Q, self.H
        self.h0 = m8(at.c * H)
        self.a0, self.b0 = m8(at.x * E), m8(Q + at.y * E)
        self.a1, self.b1 = m8(self.a0 + at.y * F), m8(self.b0 + at.x * F)
        self.stage = 0
        self.copies = []
        self.sem = 0

    def add(self, src, dst, dev):
        self.copies.append(rcopy(src, dst, self.ss.at[self.sem], self.rs.at[self.sem], dev))
        self.sem += 1

    def zat(self, ref, k):
        K = self.K
        return ref.at[pl.ds(m8((k // 2) * K), K), pl.ds(pl.multiple_of(lax.rem(k, 2) * 128, 128), 128)]

    def step(self):
        at, H, Q, E, F = self.at, self.H, self.Q, self.E, self.F
        gref, rx0, rx1, rx2, rx3, zb, zo, o = (
            self.gref, self.rx0, self.rx1, self.rx2, self.rx3, self.zb, self.zo, self.o,
        )
        h0, a0, b0, a1, b1 = self.h0, self.a0, self.b0, self.a1, self.b1
        for cp in self.copies:
            cp.wait()
        self.copies = []
        k = self.stage
        self.stage += 1
        if k == 0:
            self.add(self.src.at[pl.ds(m8((1 - at.c) * H), H)], rx0, at.core)
        elif k == 1:
            add_rows(gref, 0, self.src, h0, [rx0], H)
            for d in range(1, 4):
                xi, yi = lax.rem(at.x + d, 4), lax.rem(at.y + d, 4)
                self.add(gref.at[pl.ds(m8(xi * E), E)], rx1.at[0, d - 1], at.xp[d - 1])
                self.add(gref.at[pl.ds(m8(Q + yi * E), E)], rx1.at[1, d - 1], at.yp[d - 1])
        elif k == 2:
            add_rows(gref, a0, gref, a0, [rx1.at[0, d] for d in range(3)], E)
            add_rows(gref, b0, gref, b0, [rx1.at[1, d] for d in range(3)], E)
            for d in range(1, 4):
                xi, yi = lax.rem(at.x + d, 4), lax.rem(at.y + d, 4)
                self.add(gref.at[pl.ds(m8(a0 + yi * F), F)], rx2.at[0, d - 1], at.yp[d - 1])
                self.add(gref.at[pl.ds(m8(b0 + xi * F), F)], rx2.at[1, d - 1], at.xp[d - 1])
        elif k == 3:
            add_rows(zb, 0, gref, a1, [rx2.at[0, d] for d in range(3)], F)
            add_rows(zb, F, gref, b1, [rx2.at[1, d] for d in range(3)], F)
            for d in range(1, 8):
                self.add(self.zat(zb, lax.rem(at.z + d, 8)), rx3.at[d - 1], at.zp[d - 1])
        elif k == 4:
            acc = self.zat(zb, at.z)[...]
            for d in range(7):
                acc = acc + rx3[d]
            mine = self.zat(zo, at.z)
            mine[...] = acc
            for d in range(1, 8):
                self.add(mine, mine, at.zp[d - 1])
        elif k == 5:
            o[pl.ds(m8(h0 + a1), F), :] = zo[0:F, :]
            o[pl.ds(m8(h0 + b1), F), :] = zo[F : 2 * F, :]
            ra, rb = o.at[pl.ds(m8(h0 + a1), F)], o.at[pl.ds(m8(h0 + b1), F)]
            for d in range(1, 4):
                self.add(ra, ra, at.yp[d - 1])
                self.add(rb, rb, at.xp[d - 1])
        elif k == 6:
            ra, rb = o.at[pl.ds(m8(h0 + a0), E)], o.at[pl.ds(m8(h0 + b0), E)]
            for d in range(1, 4):
                self.add(ra, ra, at.xp[d - 1])
                self.add(rb, rb, at.yp[d - 1])
        elif k == 7:
            half = o.at[pl.ds(h0, H)]
            self.add(half, half, at.core)
        for cp in self.copies:
            cp.start()


def small_scratch(r):
    return [
        pltpu.VMEM((8, r, 128), f32),
        pltpu.VMEM((8, r, 128), f32),
        pltpu.VMEM((7, r, 128), f32),
        pltpu.VMEM((8, r, 128), f32),
        pltpu.SemaphoreType.DMA((3, 7)),
        pltpu.SemaphoreType.DMA((3, 7)),
    ]


def big_scratch(n):
    H, E, F = n // 2, n // 16, n // 64
    return [
        pltpu.VMEM((n, 256), f32),
        pltpu.VMEM((H, 256), f32),
        pltpu.VMEM((H, 256), f32),
        pltpu.VMEM((2, 3, E, 256), f32),
        pltpu.VMEM((2, 3, F, 256), f32),
        pltpu.VMEM((7, F // 2, 128), f32),
        pltpu.VMEM((2 * F, 256), f32),
        pltpu.VMEM((2 * F, 256), f32),
        pltpu.SemaphoreType.DMA((40,)),
        pltpu.SemaphoreType.DMA((40,)),
    ]


def dg(a, b, ca, cb, precision=None):
    return lax.dot_general(a, b, (((ca,), (cb,)), ((), ())), preferred_element_type=f32, precision=precision)


def exact(a, b, ca, cb):
    return dg(a, b, ca, cb, HIGHEST)


def split(v):
    hi = v.astype(bf16)
    return hi, (v - hi.astype(f32)).astype(bf16)


def iota(shape, dim):
    return lax.broadcasted_iota(jnp.int32, shape, dim)


def block_sum(v, ones):
    out = []
    for half in range(2):
        hi, lo = split(v[:, half * 256 : (half + 1) * 256])
        out.append(dg(hi, ones, 1, 0) + dg(lo, ones, 1, 0))
    return jnp.concatenate(out, axis=1)


def spread_heads(t):
    lanes = iota((HEAD_DIM, HM), 1) // SLICES
    return jnp.concatenate([jnp.where(lanes == h, t, 0.0) for h in range(HEADS)], axis=0)


def gather_heads(ref):
    lanes = iota((HEAD_DIM, HM), 1) // SLICES
    acc = jnp.zeros((HEAD_DIM, HM), f32)
    for h in range(HEADS):
        acc = jnp.where(lanes == h, ref[h * HEAD_DIM : (h + 1) * HEAD_DIM, :], acc)
    return acc


def mean_rows(v):
    return jnp.sum(v, axis=1, keepdims=True) * (1.0 / D)


def norm_parts(v):
    centred = v - mean_rows(v)
    rstd = lax.rsqrt(mean_rows(centred * centred) + EPS)
    return centred * rstd, rstd


def norm_back(dn, xhat, rstd, gain):
    dxh = dn * gain
    return rstd * (dxh - mean_rows(dxh) - xhat * mean_rows(dxh * xhat))


def fold8(v):
    return jnp.sum(v.reshape(v.shape[0] // 8, 8, v.shape[1]), axis=0)


def tiles(body):
    def step(i, _):
        body(pl.ds(pl.multiple_of(i * TILE, TILE), TILE))
        return 0

    lax.fori_loop(0, CELLS // TILE, step, 0)


def main_kernel(
    temp_ref, x_ref, dy_ref, gain1_ref, wmid_ref, wfeat_ref, ws_ref, wq_ref, wk_ref, wv_ref, wout_ref, gain2_ref,
    wup_ref, wdown_ref,
    cells_ref, o1_ref, o2_ref,
    normed_ref, mid_ref, feat_ref, l_ref, w_ref, wb_ref, spread_ref, normed2_ref, hidden_ref, du_ref, dstate_ref,
    dsb_ref, dsp_ref, dw2_ref, bds_ref, bdm_ref, bdw_ref, big_acc, mid_acc, row_acc, p_ref,
    s1, so1, s1a, s1b, ss1, rs1, s2, so2, s2a, s2b, ss2, rs2,
    g1, g1a, g1b, g1c, g1d, g1e, g1f, g1g, ss3, rs3, g2, g2a, g2b, g2c, g2d, g2e, g2f, g2g, ss4, rs4,
):
    at = Place()
    everyone = at.gp + at.zp + at.yp
    sem = pltpu.get_barrier_semaphore()
    for dev in everyone:
        pl.semaphore_signal(sem, inc=1, device_id=dev, device_id_type=MESH)
    sum1 = SmallSum(at, s1, so1, s1a, s1b, ss1, rs1)
    sum2 = SmallSum(at, s2, so2, s2a, s2b, ss2, rs2)
    big1 = BigSum(N1, at, g1, o1_ref, (g1a, g1b, g1c, g1d, g1e, g1f, g1g), ss3, rs3)
    big2 = BigSum(N2, at, g2, o2_ref, (g2a, g2b, g2c, g2d, g2e, g2f, g2g), ss4, rs4)

    head_of_lane = iota((1, HM), 1) // SLICES
    temp = jnp.zeros((1, HM), f32)
    for h in range(HEADS):
        temp = jnp.where(head_of_lane == h, temp_ref[h], temp)
    inv_temp = 1.0 / temp
    ones = (iota((256, 256), 0) // SLICES == iota((256, 256), 1) // SLICES).astype(f32).astype(bf16)
    place = (iota((SLICES, HM), 0) == lax.rem(iota((SLICES, HM), 1), SLICES)).astype(f32)
    wide = dg(ws_ref[...], place.astype(bf16), 1, 0)
    bds_ref[...] = spread_heads(wide).astype(bf16)
    gain1 = gain1_ref[...]
    gain2 = gain2_ref[...]

    big_acc[...] = jnp.zeros_like(big_acc)
    row_acc[...] = jnp.zeros_like(row_acc)

    def part_a(r):
        xhat, _ = norm_parts(x_ref[r, :].astype(f32))
        normed = (xhat * gain1).astype(bf16)
        normed_ref[r, :] = normed
        mid = dg(normed, wmid_ref[...], 1, 0)
        feat = dg(normed, wfeat_ref[...], 1, 0).astype(bf16)
        hi, lo = split(mid)
        mid_ref[r, :] = hi
        feat_ref[r, :] = feat
        logits = (dg(hi, bds_ref[...], 1, 0) + dg(lo, bds_ref[...], 1, 0)) * inv_temp
        l_ref[r, :] = logits
        e = jnp.exp(logits)
        w = e / block_sum(e, ones)
        w_ref[r, :] = w
        wb = w.astype(bf16)
        wb_ref[r, :] = wb
        big_acc[...] += dg(feat, wb, 0, 0)
        row_acc[...] += fold8(w)

    tiles(part_a)
    tt = gather_heads(big_acc)
    tot = row_acc[...]
    for j in range(8):
        lanes = slice((j // 2) * 128, (j // 2 + 1) * 128)
        s1[j, 0:16, :] = tt[(j % 2) * 16 : (j % 2 + 1) * 16, lanes]
        s1[j, 16:24, :] = tot[:, lanes]

    pl.semaphore_wait(sem, len(everyone))
    sum1.step()
    sum1.step()
    sum1.step()
    sum1.wait()

    wq, wk, wv = (r[...].astype(f32) for r in (wq_ref, wk_ref, wv_ref))
    scale = HEAD_DIM**-0.5
    same = iota((128, 128), 0) // SLICES == iota((128, 128), 1) // SLICES
    mix = []
    kept = []
    for b in range(4):
        total = jnp.sum(so1[2 * b, 16:24, :], axis=0, keepdims=True)
        tok = jnp.concatenate([so1[2 * b, 0:16, :], so1[2 * b + 1, 0:16, :]], axis=0) / total
        q = exact(wq, tok, 0, 0)
        k = exact(wk, tok, 0, 0)
        v = exact(wv, tok, 0, 0)
        sc = exact(q, k, 0, 0) * scale
        e = jnp.where(same, jnp.exp(jnp.where(same, sc, 0.0)), 0.0)
        prob = e / jnp.sum(e, axis=1, keepdims=True)
        p_ref[b] = prob
        mix.append(exact(v, prob, 1, 1))
        kept.append((total, tok, q, k, v))
    hi, lo = split(spread_heads(jnp.concatenate(mix, axis=1)))
    bdm_ref[0] = hi
    bdm_ref[1] = lo

    big_acc[...] = jnp.zeros_like(big_acc)
    row_acc[...] = jnp.zeros_like(row_acc)

    def part_b(r):
        wb = wb_ref[r, :]
        sp = (dg(wb, bdm_ref[0], 1, 1) + dg(wb, bdm_ref[1], 1, 1)).astype(bf16)
        spread_ref[r, :] = sp
        state = x_ref[r, :].astype(f32) + dg(sp, wout_ref[...], 1, 0)
        xhat, rstd = norm_parts(state)
        normed = (xhat * gain2).astype(bf16)
        normed2_ref[r, :] = normed
        dy = dy_ref[r, :]
        dn = jnp.zeros((TILE, D), f32)
        for j in range(4):
            cols = slice(j * 256, (j + 1) * 256)
            u = dg(normed, wup_ref[:, cols], 1, 0)
            u2 = u * u
            t = jnp.tanh(u * (GELU_C + (GELU_C * GELU_A) * u2))
            half = 0.5 + 0.5 * t
            hidden_ref[r, cols] = (u * half).astype(bf16)
            slope = half + u * half * (1.0 - t) * (GELU_C + (3.0 * GELU_C * GELU_A) * u2)
            dh = dg(dy, wdown_ref[cols, :], 1, 1).astype(bf16).astype(f32)
            du = (dh * slope).astype(bf16)
            du_ref[r, cols] = du
            dn = dn + dg(du, wup_ref[:, cols], 1, 1)
        dn = dn.astype(bf16).astype(f32)
        row_acc[:, 0:256] += fold8(dn * xhat)
        ds = dy.astype(f32) + norm_back(dn, xhat, rstd, gain2)
        dstate_ref[r, :] = ds
        dsb = ds.astype(bf16)
        dsb_ref[r, :] = dsb
        dsp = dg(dsb, wout_ref[...], 1, 1).astype(bf16)
        dsp_ref[r, :] = dsp
        big_acc[...] += dg(dsp, wb, 0, 0)

    tiles(part_b)
    dmt = gather_heads(big_acc)
    for j in range(8):
        s2[j] = dmt[(j % 2) * 16 : (j % 2 + 1) * 16, (j // 2) * 128 : (j // 2 + 1) * 128]
    g_gain2 = jnp.sum(row_acc[:, 0:256], axis=0, keepdims=True)
    sum2.step()

    for j in range(4):
        cols = slice(j * 256, (j + 1) * 256)
        g1[j * 256 : (j + 1) * 256, :] = dg(hidden_ref[:, cols], dy_ref[...], 0, 0)
    sum2.step()
    for j in range(4):
        cols = slice(j * 256, (j + 1) * 256)
        g1[1024 + j * 256 : 1280 + j * 256, :] = dg(normed2_ref[...], du_ref[:, cols], 0, 0)
    big1.step()

    def part_dw(r):
        dsp = dsp_ref[r, :]
        dw2_ref[r, :] = dg(dsp, bdm_ref[0], 1, 0) + dg(dsp, bdm_ref[1], 1, 0)

    tiles(part_dw)
    g2[512:768, :] = dg(spread_ref[...], dsb_ref[...], 0, 0)
    sum2.step()
    big1.step()
    sum2.wait()

    gq = jnp.zeros((HEAD_DIM, HEAD_DIM), f32)
    gk, gv = gq, gq
    dwt, dtot = [], []
    for b in range(4):
        total, tok, q, k, v = kept[b]
        prob = p_ref[b]
        dm = jnp.concatenate([so2[2 * b], so2[2 * b + 1]], axis=0)
        dp = exact(dm, v, 0, 0)
        dsc = prob * (dp - jnp.sum(prob * dp, axis=1, keepdims=True)) * scale
        dq = exact(k, dsc, 1, 1)
        dk = exact(q, dsc, 1, 0)
        dv = exact(dm, prob, 1, 0)
        gq = gq + exact(tok, dq, 1, 1)
        gk = gk + exact(tok, dk, 1, 1)
        gv = gv + exact(tok, dv, 1, 1)
        dtok = exact(wq, dq, 1, 0) + exact(wk, dk, 1, 0) + exact(wv, dv, 1, 0)
        dtok = dtok / total
        dwt.append(dtok)
        dtot.append(-jnp.sum(dtok * tok, axis=0, keepdims=True))
    hi, lo = split(spread_heads(jnp.concatenate(dwt, axis=1)))
    bdw_ref[0] = hi
    bdw_ref[1] = lo
    d_totals = jnp.concatenate(dtot, axis=1)

    big_acc[...] = jnp.zeros_like(big_acc)
    mid_acc[...] = jnp.zeros_like(mid_acc)
    row_acc[...] = jnp.zeros_like(row_acc)
    g2[0:512, :] = jnp.zeros((512, 256), f32)

    def part_c(r):
        w = w_ref[r, :]
        wb = wb_ref[r, :]
        feat = feat_ref[r, :]
        normed = normed_ref[r, :]
        dfeat = (dg(wb, bdw_ref[0], 1, 1) + dg(wb, bdw_ref[1], 1, 1)).astype(bf16)
        dw = dw2_ref[r, :] + dg(feat, bdw_ref[0], 1, 0) + dg(feat, bdw_ref[1], 1, 0) + d_totals
        dl = w * (dw - block_sum(w * dw, ones))
        row_acc[...] += fold8(dl * l_ref[r, :])
        dlt = (dl * inv_temp).astype(bf16)
        dmid = dg(dlt, bds_ref[...], 1, 1).astype(bf16)
        big_acc[...] += dg(mid_ref[r, :], dlt, 0, 0)
        g2[0:256, :] += dg(normed, dfeat, 0, 0)
        g2[256:512, :] += dg(normed, dmid, 0, 0)
        dn = dg(dmid, wmid_ref[...], 1, 1).astype(bf16).astype(f32) + dg(dfeat, wfeat_ref[...], 1, 1).astype(
            bf16
        ).astype(f32)
        dn = dn.astype(bf16).astype(f32)
        xhat, rstd = norm_parts(x_ref[r, :].astype(f32))
        mid_acc[...] += fold8(dn * xhat)
        cells_ref[r, :] = (norm_back(dn, xhat, rstd, gain1) + dstate_ref[r, :]).astype(bf16)

    tiles(part_c)
    big1.step()

    first = (lax.axis_index("point") == 0).astype(f32)
    g2[SMALL:N2, :] = jnp.zeros((N2 - SMALL, 256), f32)
    pick = (iota((HM, 256), 0) // SLICES == iota((HM, 256), 1)).astype(f32)
    inv8 = jnp.zeros((1, 256), f32)
    for h in range(HEADS):
        inv8 = jnp.where(iota((1, 256), 1) == h, 1.0 / temp_ref[h], inv8)
    g_temp = jnp.sum(exact(row_acc[...], pick, 1, 0), axis=0, keepdims=True) * (-inv8)
    g2[SMALL : SMALL + 1, :] = jnp.sum(mid_acc[...], axis=0, keepdims=True)
    g2[SMALL + 1 : SMALL + 2, :] = g_gain2
    g2[SMALL + 2 : SMALL + 3, :] = g_temp
    g2[SMALL + 8 : SMALL + 40, 0:64] = exact(gather_heads(big_acc), place, 1, 1)
    g2[SMALL + 8 : SMALL + 40, 128:160] = gq * first
    g2[SMALL + 40 : SMALL + 72, 0:32] = gk * first
    g2[SMALL + 40 : SMALL + 72, 128:160] = gv * first
    big2.step()
    for _ in range(4):
        big1.step()
        big2.step()
    big1.step()
    big2.step()
    big1.step()
    big2.step()
    big2.step()
    big2.step()
    big2.step()


def out_kernel(
    cells_ref, o1, o2, cells_out, gain1, mid, feat, slc, temp, wq, wk, wv, wout, gain2, up, down,
):
    cells_out[...] = cells_ref[...]
    down[...] = o1[0:1024, :]
    for j in range(4):
        up[:, j * 256 : (j + 1) * 256] = o1[1024 + j * 256 : 1280 + j * 256, :]
    feat[...] = o2[0:256, :]
    mid[...] = o2[256:512, :]
    wout[...] = o2[512:768, :]
    gain1[...] = o2[SMALL : SMALL + 1, :]
    gain2[...] = o2[SMALL + 1 : SMALL + 2, :]
    temp[...] = o2[SMALL + 2 : SMALL + 3, 0:8]
    slc[...] = o2[SMALL + 8 : SMALL + 40, 0:64]
    wq[...] = o2[SMALL + 8 : SMALL + 40, 128:160]
    wk[...] = o2[SMALL + 40 : SMALL + 72, 0:32]
    wv[...] = o2[SMALL + 40 : SMALL + 72, 128:160]


def vmem(count):
    return [pl.BlockSpec(memory_space=pltpu.VMEM)] * count


def on_device(x, dy, gain1, wmid, wfeat, ws, temp, wq, wk, wv, wout, gain2, wup, wdown):
    sds = jax.ShapeDtypeStruct
    cells, o1, o2 = pl.pallas_call(
        main_kernel,
        out_shape=(sds((CELLS, D), bf16), sds((N1, 256), f32), sds((N2, 256), f32)),
        in_specs=[pl.BlockSpec(memory_space=pltpu.SMEM)] + vmem(13),
        out_specs=vmem(3),
        scratch_shapes=[
            pltpu.VMEM((CELLS, D), bf16),
            pltpu.VMEM((CELLS, D), bf16),
            pltpu.VMEM((CELLS, D), bf16),
            pltpu.VMEM((CELLS, HM), f32),
            pltpu.VMEM((CELLS, HM), f32),
            pltpu.VMEM((CELLS, HM), bf16),
            pltpu.VMEM((CELLS, D), bf16),
            pltpu.VMEM((CELLS, D), bf16),
            pltpu.VMEM((CELLS, FF), bf16),
            pltpu.VMEM((CELLS, FF), bf16),
            pltpu.VMEM((CELLS, D), f32),
            pltpu.VMEM((CELLS, D), bf16),
            pltpu.VMEM((CELLS, D), bf16),
            pltpu.VMEM((CELLS, HM), f32),
            pltpu.VMEM((D, HM), bf16),
            pltpu.VMEM((2, D, HM), bf16),
            pltpu.VMEM((2, D, HM), bf16),
            pltpu.VMEM((D, HM), f32),
            pltpu.VMEM((8, D), f32),
            pltpu.VMEM((8, HM), f32),
            pltpu.VMEM((4, 128, 128), f32),
        ]
        + small_scratch(24)
        + small_scratch(16)
        + big_scratch(N1)
        + big_scratch(N2),
        compiler_params=pltpu.CompilerParams(
            collective_id=0, has_side_effects=True, vmem_limit_bytes=56 * 2**20
        ),
    )(
        temp, x[0], dy[0], gain1.reshape(1, D), wmid, wfeat, ws, wq, wk, wv, wout, gain2.reshape(1, D), wup, wdown,
    )
    outs = pl.pallas_call(
        out_kernel,
        out_shape=(
            sds((CELLS, D), bf16), sds((1, D), f32), sds((D, D), f32), sds((D, D), f32),
            sds((HEAD_DIM, SLICES), f32), sds((1, HEADS), f32), sds((HEAD_DIM, HEAD_DIM), f32),
            sds((HEAD_DIM, HEAD_DIM), f32), sds((HEAD_DIM, HEAD_DIM), f32), sds((D, D), f32), sds((1, D), f32),
            sds((D, FF), f32), sds((FF, D), f32),
        ),
        in_specs=vmem(3),
        out_specs=vmem(13),
        compiler_params=pltpu.CompilerParams(vmem_limit_bytes=24 * 2**20),
    )(cells, o1, o2)
    outs = list(outs)
    outs[0] = outs[0][None]
    outs[1] = outs[1].reshape(D)
    outs[5] = outs[5].reshape(HEADS)
    outs[10] = outs[10].reshape(D)
    return tuple(outs)


def solution(mesh):
    return jax.shard_map(
        on_device,
        mesh=mesh,
        in_specs=(P("dp", "point", None), P("dp", "point", None)) + (P(),) * 12,
        out_specs=(P("dp", "point", None),) + (P(),) * 12,
        check_vma=False,
    )
```

time: 678 us -> 99.8 us (0.15)
  waiting for transfers between devices: 383 us -> 0 us
  blocking collectives: 217 us -> 0 us
  Pallas kernels: 0 us -> 95.1 us
  matrix products: 40.9 us -> 0 us
  between operations: 14.6 us -> 0.67 us
  local copies, waits for them, and re-layouts: 16.7 us -> 3.8 us
    psum x3 -> x0, waiting for transfers between devices: 383 us -> none  [the longest x1 169 us: on_device(): d_tokens = lax.psum(d_tokens, 'point')]
    psum x3 -> x0, blocking collectives: 217 us -> none  [the longest x1 128 us: on_device(): lax.psum((aggregated_states, partition_mass), 'point')]
    pallas_call x0 -> x2, Pallas kernels: none -> 95.1 us  [the longest x1 93.2 us: on_device(): pl.pallas_call(main_kernel, out_shape=(sds((CELLS, D), bf16), sds((N1, 25...]
    dot_general x38 -> x0, matrix products: 40.9 us -> none  [the longest x3 6.1 us: partition_share(): jnp.einsum('che,em->chm', middle, partition_score_matrix.astype(jnp.float...]
    unnamed x124 -> x6, local copies, waits for them, and re-layouts: 16.7 us -> 3.8 us
  transfers between devices with their start and end apart: 3 -> 0, of which waited for: 3 -> 0; matrix products, arithmetic and copies ran while one was open for 1% -> 0% of each run, Pallas kernels for 0% -> 0%
where the time goes in v2:
time: 99.8 us; the launch traced here: 99.6 us
  Pallas kernels  95.1 us (95%)
  local copies, waits for them, and re-layouts  3.8 us (4%)
    pallas_call x1, Pallas kernels, on_device(): pl.pallas_call(main_kernel, out_shape=(sds((CELLS, D), bf16), sds((N1, 25...  93.2 us
    unnamed x6, local copies, waits for them, and re-layouts  3.8 us

profile of v2, /device:TPU:1, one launch (start us, length us, event | category | flops | bytes accessed | tf_op | source)
XLA Modules:
  0.0 99.6 jit_solution(3804309934532640662)
XLA Ops:
  0.7 93.2 %shard_map.237 = (bf16[768,256]{1,0:T(8,128)(2,1)}, f32[2048,256]{1,0:T(8,128)}, f32[1024,256]{1,0:T(8,128)}) custom-call(f32[8]{0:T(128)} %temp_ref.1, bf16[768,256]{1,0:T(8,128)(2,1)} %bitcast.8, bf16[768,256]{1,0:T(8,128)(2,1)} %bitcast.9, f32[1,256]{1,0:T(1,128)} %bitcast.10, bf16[256,256]{1,0:T(8,128)(2,1)} %wmid_ref.1, bf16[256,256]{1,0:T(8,128)(2,1)} %wfeat_ref.1, ...), custom_call_target="tpu_custom_call" | custom-call | tf_op jit(solution)/shard_map/pallas_call | solution.py:537
  93.8 0.0 copy-start
  93.9 1.6 %copy-done = f32[2048,256]{1,0:T(8,128)S(1)} copy-done((f32[2048,256]{1,0:T(8,128)S(1)}, f32[2048,256]{1,0:T(8,128)}, u32[]{:S(2)}) %copy-start) | copy-done | bytes 2097176
  95.4 0.0 copy-start.1
  95.4 1.2 %copy-done.1 = f32[1024,256]{1,0:T(8,128)S(1)} copy-done((f32[1024,256]{1,0:T(8,128)S(1)}, f32[1024,256]{1,0:T(8,128)}, u32[]{:S(2)}) %copy-start.1) | copy-done | bytes 1048600
  96.7 0.0 copy-start.2
  96.7 1.0 copy-done.2
  97.7 1.9 %shard_map.238 = (bf16[768,256]{1,0:T(8,128)(2,1)}, f32[1,256]{1,0:T(1,128)}, f32[256,256]{1,0:T(8,128)}, f32[256,256]{1,0:T(8,128)}, f32[32,64]{1,0:T(8,128)}, ...) custom-call(bf16[768,256]{1,0:T(8,128)(2,1)S(1)} %copy-done.2, ...), custom_call_target="tpu_custom_call" | custom-call | tf_op jit(solution)/shard_map/pallas_call | solution.py:575
Async XLA Ops:
  93.8 1.6 %copy-start = (f32[2048,256]{1,0:T(8,128)S(1)}, f32[2048,256]{1,0:T(8,128)}, u32[]{:S(2)}) copy-start(f32[2048,256]{1,0:T(8,128)} %get-tuple-element.30.o1) | copy-start | bytes 6291460
  95.4 1.2 %copy-start.1 = (f32[1024,256]{1,0:T(8,128)S(1)}, f32[1024,256]{1,0:T(8,128)}, u32[]{:S(2)}) copy-start(f32[1024,256]{1,0:T(8,128)} %get-tuple-element.31.o2) | copy-start | bytes 3145732
  96.7 1.0 copy-start.2

commit v3 on v2

v3 whole, which is shorter than its diff:
```python
import functools
import jax
import jax.numpy as jnp
from jax import lax
from jax.experimental import pallas as pl
from jax.experimental.pallas import tpu as pltpu
from jax.sharding import PartitionSpec as P

MESH = pl.DeviceIdType.MESH
HIGHEST = lax.Precision.HIGHEST
f32 = jnp.float32
bf16 = jnp.bfloat16

CELLS = 768
D = 256
FF = 1024
HEADS = 8
SLICES = 64
HEAD_DIM = 32
HM = HEADS * SLICES
EPS = 1e-05
N1 = 2048
N2 = 512
N3 = 384
SMALL = 256
GELU_C = 0.7978845608028654
GELU_A = 0.044715


def rcopy(src, dst, ss, rs, dev):
    return pltpu.make_async_remote_copy(
        src_ref=src, dst_ref=dst, send_sem=ss, recv_sem=rs, device_id=dev, device_id_type=MESH
    )


def m8(v):
    return pl.multiple_of(v, 8)


class Place:
    def __init__(self):
        self.y = lax.axis_index("dp")
        p = lax.axis_index("point")
        self.z = p // 8
        self.g = lax.rem(p, 8)
        self.x = self.g // 2
        self.c = lax.rem(self.g, 2)
        z, x, c, g, y = self.z, self.x, self.c, self.g, self.y
        self.core = {"point": z * 8 + x * 2 + (1 - c)}
        self.gp = [{"point": z * 8 + lax.rem(g + d, 8)} for d in range(1, 8)]
        self.zp = [{"point": lax.rem(z + d, 8) * 8 + g} for d in range(1, 8)]
        self.xp = [{"point": z * 8 + lax.rem(x + d, 4) * 2 + c} for d in range(1, 4)]
        self.yp = [{"dp": lax.rem(y + d, 4)} for d in range(1, 4)]
        self.xyp = [
            {"dp": lax.rem(y + d % 4, 4), "point": z * 8 + lax.rem(x + d // 4, 4) * 2 + c} for d in range(1, 16)
        ]
        far = [self.xyp[d - 1] for d in range(1, 16) if d % 4]
        self.everyone = self.gp + self.zp + far


class Stage:
    def __init__(self, ss, rs):
        self.ss, self.rs, self.k, self.pending = ss, rs, -1, None
        self.copies = []

    def wait(self):
        if self.pending is not None:
            self.pending.wait_send()
            self.pending.wait_recv()
        self.pending = None
        self.copies = []

    def begin(self):
        self.wait()
        self.k += 1
        return self.k

    def add(self, src, dst, dev):
        rcopy(src, dst, self.ss.at[self.k], self.rs.at[self.k], dev).start()

    def total(self, ref, dev):
        self.pending = rcopy(ref, ref, self.ss.at[self.k], self.rs.at[self.k], dev)


class SmallSum(Stage):
    def __init__(self, at, s, o, rx1, rx2, ss, rs):
        super().__init__(ss, rs)
        self.at, self.s, self.o, self.rx1, self.rx2 = at, s, o, rx1, rx2

    def step(self):
        at, s, o, rx1, rx2 = self.at, self.s, self.o, self.rx1, self.rx2
        k = self.begin()
        if k == 0:
            for d in range(1, 8):
                self.add(s.at[lax.rem(at.g + d, 8)], rx1.at[d - 1], at.gp[d - 1])
            self.total(rx1, at.gp[0])
        elif k == 1:
            acc = s[at.g]
            for d in range(7):
                acc = acc + rx1[d]
            rx2[at.z] = acc
            mine = rx2.at[at.z]
            for d in range(7):
                self.add(mine, mine, at.zp[d])
            self.total(rx1, at.zp[0])
        elif k == 2:
            acc = rx2[0]
            for d in range(1, 8):
                acc = acc + rx2[d]
            o[at.g] = acc
            mine = o.at[at.g]
            for d in range(7):
                self.add(mine, mine, at.gp[d])
            self.total(rx1, at.gp[0])


def add_rows(dst, d0, base, b0, srcs, rows):
    t = min(rows, 64)

    def body(i, _):
        o = pl.multiple_of(i * t, t)
        acc = base[pl.ds(m8(b0 + o), t), :]
        for s in srcs:
            acc = acc + s[pl.ds(o, t), :]
        dst[pl.ds(m8(d0 + o), t), :] = acc
        return 0

    lax.fori_loop(0, rows // t, body, 0)


class BigSum(Stage):
    def __init__(self, n, at, src, o, bufs, ss, rs):
        super().__init__(ss, rs)
        self.n, self.at, self.src, self.o = n, at, src, o
        self.gref, self.rx0, self.rx1, self.rx2, self.rx3, self.zb, self.zo = bufs
        self.H, self.Q, self.E, self.F = n // 2, n // 4, n // 16, n // 64
        self.K = self.F // 2
        E, F, Q, H = self.E, self.F, self.Q, self.H
        self.h0 = m8(at.c * H)
        self.a0, self.b0 = m8(at.x * E), m8(Q + at.y * E)
        self.a1, self.b1 = m8(self.a0 + at.y * F), m8(self.b0 + at.x * F)

    def zat(self, ref, k):
        K = self.K
        return ref.at[pl.ds(m8((k // 2) * K), K), pl.ds(pl.multiple_of(lax.rem(k, 2) * 128, 128), 128)]

    def step(self):
        at, H, Q, E, F = self.at, self.H, self.Q, self.E, self.F
        gref, rx0, rx1, rx2, rx3, zb, zo, o = (
            self.gref, self.rx0, self.rx1, self.rx2, self.rx3, self.zb, self.zo, self.o,
        )
        h0, a0, b0, a1, b1 = self.h0, self.a0, self.b0, self.a1, self.b1
        k = self.begin()
        if k == 0:
            self.add(self.src.at[pl.ds(m8((1 - at.c) * H), H)], rx0, at.core)
            self.total(rx0, at.core)
        elif k == 1:
            add_rows(gref, 0, self.src, h0, [rx0], H)
            for d in range(1, 4):
                xi, yi = lax.rem(at.x + d, 4), lax.rem(at.y + d, 4)
                self.add(gref.at[pl.ds(m8(xi * E), E)], rx1.at[0, d - 1], at.xp[d - 1])
                self.add(gref.at[pl.ds(m8(Q + yi * E), E)], rx1.at[1, d - 1], at.yp[d - 1])
            self.total(rx1, at.xp[0])
        elif k == 2:
            add_rows(gref, a0, gref, a0, [rx1.at[0, d] for d in range(3)], E)
            add_rows(gref, b0, gref, b0, [rx1.at[1, d] for d in range(3)], E)
            for d in range(1, 4):
                xi, yi = lax.rem(at.x + d, 4), lax.rem(at.y + d, 4)
                self.add(gref.at[pl.ds(m8(a0 + yi * F), F)], rx2.at[0, d - 1], at.yp[d - 1])
                self.add(gref.at[pl.ds(m8(b0 + xi * F), F)], rx2.at[1, d - 1], at.xp[d - 1])
            self.total(rx2, at.xp[0])
        elif k == 3:
            add_rows(zb, 0, gref, a1, [rx2.at[0, d] for d in range(3)], F)
            add_rows(zb, F, gref, b1, [rx2.at[1, d] for d in range(3)], F)
            for d in range(1, 8):
                self.add(self.zat(zb, lax.rem(at.z + d, 8)), rx3.at[d - 1], at.zp[d - 1])
            self.total(rx3, at.zp[0])
        elif k == 4:
            acc = self.zat(zb, at.z)[...]
            for d in range(7):
                acc = acc + rx3[d]
            mine = self.zat(zo, at.z)
            mine[...] = acc
            for d in range(1, 8):
                self.add(mine, mine, at.zp[d - 1])
            self.total(rx3, at.zp[0])
        elif k == 5:
            o[pl.ds(m8(h0 + a1), F), :] = zo[0:F, :]
            o[pl.ds(m8(h0 + b1), F), :] = zo[F : 2 * F, :]
            ra, rb = o.at[pl.ds(m8(h0 + a1), F)], o.at[pl.ds(m8(h0 + b1), F)]
            for d in range(1, 4):
                self.add(ra, ra, at.yp[d - 1])
                self.add(rb, rb, at.xp[d - 1])
            self.total(rx2, at.xp[0])
        elif k == 6:
            ra, rb = o.at[pl.ds(m8(h0 + a0), E)], o.at[pl.ds(m8(h0 + b0), E)]
            for d in range(1, 4):
                self.add(ra, ra, at.xp[d - 1])
                self.add(rb, rb, at.yp[d - 1])
            self.total(rx1, at.xp[0])
        elif k == 7:
            half = o.at[pl.ds(h0, H)]
            self.add(half, half, at.core)
            self.total(rx0, at.core)


class MidSum(Stage):
    def __init__(self, n, at, src, o, bufs, ss, rs):
        super().__init__(ss, rs)
        self.n, self.at, self.src, self.o = n, at, src, o
        self.gref, self.rx0, self.rx1, self.rx2 = bufs
        self.r = n // 16

    def lanes(self, ref, c):
        return ref.at[:, pl.ds(pl.multiple_of(c * 128, 128), 128)]

    def step(self):
        at, r, gref, rx0, rx1, rx2 = self.at, self.r, self.gref, self.rx0, self.rx1, self.rx2
        k = self.begin()
        own = m8((at.x * 4 + at.y) * r)
        if k == 0:
            self.add(self.lanes(self.src, 1 - at.c), rx0, at.core)
            self.total(rx0, at.core)
        elif k == 1:
            gref[...] = self.lanes(self.src, at.c)[...] + rx0[...]
            for d in range(1, 16):
                to = lax.rem(at.x + d // 4, 4) * 4 + lax.rem(at.y + d % 4, 4)
                self.add(gref.at[pl.ds(m8(to * r), r)], rx1.at[d - 1], at.xyp[d - 1])
            self.total(rx1, at.xyp[0])
        elif k == 2:
            acc = gref[pl.ds(own, r), :]
            for d in range(15):
                acc = acc + rx1[d]
            rx2[at.z] = acc
            mine = rx2.at[at.z]
            for d in range(7):
                self.add(mine, mine, at.zp[d])
            self.total(rx2.at[pl.ds(0, 7)], at.zp[0])
        elif k == 3:
            acc = rx2[0]
            for d in range(1, 8):
                acc = acc + rx2[d]
            mine = self.o.at[pl.ds(own, r), pl.ds(pl.multiple_of(at.c * 128, 128), 128)]
            mine[...] = acc
            for d in range(15):
                self.add(mine, mine, at.xyp[d])
            self.total(rx1, at.xyp[0])
        elif k == 4:
            half = self.lanes(self.o, at.c)
            self.add(half, half, at.core)
            self.total(rx0, at.core)


def mid_scratch(n):
    r = n // 16
    return [
        pltpu.VMEM((n, 256), f32),
        pltpu.VMEM((n, 128), f32),
        pltpu.VMEM((n, 128), f32),
        pltpu.VMEM((15, r, 128), f32),
        pltpu.VMEM((8, r, 128), f32),
        pltpu.SemaphoreType.DMA((5,)),
        pltpu.SemaphoreType.DMA((5,)),
    ]


def small_scratch(r):
    return [
        pltpu.VMEM((8, r, 128), f32),
        pltpu.VMEM((8, r, 128), f32),
        pltpu.VMEM((7, r, 128), f32),
        pltpu.VMEM((8, r, 128), f32),
        pltpu.SemaphoreType.DMA((3,)),
        pltpu.SemaphoreType.DMA((3,)),
    ]


def big_scratch(n):
    H, E, F = n // 2, n // 16, n // 64
    return [
        pltpu.VMEM((n, 256), f32),
        pltpu.VMEM((H, 256), f32),
        pltpu.VMEM((H, 256), f32),
        pltpu.VMEM((2, 3, E, 256), f32),
        pltpu.VMEM((2, 3, F, 256), f32),
        pltpu.VMEM((7, F // 2, 128), f32),
        pltpu.VMEM((2 * F, 256), f32),
        pltpu.VMEM((2 * F, 256), f32),
        pltpu.SemaphoreType.DMA((8,)),
        pltpu.SemaphoreType.DMA((8,)),
    ]


def dg(a, b, ca, cb, precision=None):
    return lax.dot_general(a, b, (((ca,), (cb,)), ((), ())), preferred_element_type=f32, precision=precision)


def exact(a, b, ca, cb):
    return dg(a, b, ca, cb, HIGHEST)


def split(v):
    hi = v.astype(bf16)
    return hi, (v - hi.astype(f32)).astype(bf16)


def iota(shape, dim):
    return lax.broadcasted_iota(jnp.int32, shape, dim)


def block_sum(v, ones):
    out = []
    for half in range(2):
        hi, lo = split(v[:, half * 256 : (half + 1) * 256])
        out.append(dg(hi, ones, 1, 0) + dg(lo, ones, 1, 0))
    return jnp.concatenate(out, axis=1)


def spread_heads(t):
    lanes = iota((HEAD_DIM, HM), 1) // SLICES
    return jnp.concatenate([jnp.where(lanes == h, t, 0.0) for h in range(HEADS)], axis=0)


def gather_heads(ref):
    lanes = iota((HEAD_DIM, HM), 1) // SLICES
    acc = jnp.zeros((HEAD_DIM, HM), f32)
    for h in range(HEADS):
        acc = jnp.where(lanes == h, ref[h * HEAD_DIM : (h + 1) * HEAD_DIM, :], acc)
    return acc


def mean_rows(v):
    return jnp.sum(v, axis=1, keepdims=True) * (1.0 / D)


def norm_parts(v):
    centred = v - mean_rows(v)
    rstd = lax.rsqrt(mean_rows(centred * centred) + EPS)
    return centred * rstd, rstd


def norm_back(dn, xhat, rstd, gain):
    dxh = dn * gain
    return rstd * (dxh - mean_rows(dxh) - xhat * mean_rows(dxh * xhat))


def fold8(v):
    return jnp.sum(v.reshape(v.shape[0] // 8, 8, v.shape[1]), axis=0)


def main_kernel(
    temp_ref, *rest,
):
    hbm, outs, bufs, load_sem, rest = rest[:13], rest[13:17], rest[17:30], rest[30], rest[31:]
    x_ref, dy_ref, gain1_ref, wmid_ref, wfeat_ref, ws_ref, wq_ref, wk_ref, wv_ref, wout_ref, gain2_ref, wup_ref, wdown_ref = bufs
    (
    cells_ref, o1_ref, o2_ref, o3_ref,
    ) = outs
    (
    l_ref, w_ref, du_ref, dh_ref, normed1t_ref, midt_ref, dstate_ref, dw2_ref, bds_ref, bdm_ref, bdw_ref, p_ref,
    s1, so1, s1a, s1b, ss1, rs1, s2, so2, s2a, s2b, ss2, rs2,
    g1, g1a, g1b, g1c, g1d, g1e, g1f, g1g, ss3, rs3, g2, g2a, g2b, g2c, g2d, ss4, rs4,
    g3, g3a, g3b, g3c, g3d, ss5, rs5,
    ) = rest
    loads = [pltpu.make_async_copy(hbm[i], bufs[i], load_sem.at[i]) for i in range(13)]
    for i in (0, 3, 4, 2, 5, 6, 7, 8, 9, 10, 1, 11, 12):
        loads[i].start()
    at = Place()
    everyone = at.everyone
    sem = pltpu.get_barrier_semaphore()
    for dev in everyone:
        pl.semaphore_signal(sem, inc=1, device_id=dev, device_id_type=MESH)
    sum1 = SmallSum(at, s1, so1, s1a, s1b, ss1, rs1)
    sum2 = SmallSum(at, s2, so2, s2a, s2b, ss2, rs2)
    big1 = BigSum(N1, at, g1, o1_ref, (g1a, g1b, g1c, g1d, g1e, g1f, g1g), ss3, rs3)
    mid2 = MidSum(N2, at, g2, o2_ref, (g2a, g2b, g2c, g2d), ss4, rs4)
    tail = MidSum(N3, at, g3, o3_ref, (g3a, g3b, g3c, g3d), ss5, rs5)

    for i in (0, 3, 4, 2, 5):
        loads[i].wait()

    head_of_lane = iota((1, HM), 1) // SLICES
    temp = jnp.zeros((1, HM), f32)
    for h in range(HEADS):
        temp = jnp.where(head_of_lane == h, temp_ref[h], temp)
    inv_temp = 1.0 / temp
    ones = (iota((256, 256), 0) // SLICES == iota((256, 256), 1) // SLICES).astype(f32).astype(bf16)
    place = (iota((SLICES, HM), 0) == lax.rem(iota((SLICES, HM), 1), SLICES)).astype(f32)
    wide = dg(ws_ref[...], place.astype(bf16), 1, 0)
    bds_ref[...] = spread_heads(wide).astype(bf16)
    gain1 = gain1_ref[...]

    xhat1, rstd1 = norm_parts(x_ref[...].astype(f32))
    normed1 = (xhat1 * gain1).astype(bf16)
    mid = dg(normed1, wmid_ref[...], 1, 0)
    feat = dg(normed1, wfeat_ref[...], 1, 0).astype(bf16)
    mid_hi, mid_lo = split(mid)
    logits = (dg(mid_hi, bds_ref[...], 1, 0) + dg(mid_lo, bds_ref[...], 1, 0)) * inv_temp
    l_ref[...] = logits
    e = jnp.exp(logits)
    w = e / block_sum(e, ones)
    w_ref[...] = w
    wb = w.astype(bf16)
    tt = gather_heads(dg(feat, wb, 0, 0))
    tot = fold8(w)
    for j in range(8):
        lanes = slice((j // 2) * 128, (j // 2 + 1) * 128)
        s1[j, 0:16, :] = tt[(j % 2) * 16 : (j % 2 + 1) * 16, lanes]
        s1[j, 16:24, :] = tot[:, lanes]

    pl.semaphore_wait(sem, len(everyone))
    sum1.step()
    for i in (1, 12):
        loads[i].wait()
    dy = dy_ref[...]
    for j in range(2):
        cols = slice(j * 256, (j + 1) * 256)
        dh_ref[:, cols] = dg(dy, wdown_ref[cols, :], 1, 1).astype(bf16)
    sum1.step()
    for j in range(2, 4):
        cols = slice(j * 256, (j + 1) * 256)
        dh_ref[:, cols] = dg(dy, wdown_ref[cols, :], 1, 1).astype(bf16)
    sum1.step()
    normed1t_ref[...] = normed1.T
    midt_ref[...] = mid_hi.T
    for i in (6, 7, 8, 9, 10, 11):
        loads[i].wait()
    gain2 = gain2_ref[...]
    sum1.wait()

    wq, wk, wv = (r[...].astype(f32) for r in (wq_ref, wk_ref, wv_ref))
    scale = HEAD_DIM**-0.5
    same = iota((128, 128), 0) // SLICES == iota((128, 128), 1) // SLICES
    mix = []
    kept = []
    for b in range(4):
        total = jnp.sum(so1[2 * b, 16:24, :], axis=0, keepdims=True)
        tok = jnp.concatenate([so1[2 * b, 0:16, :], so1[2 * b + 1, 0:16, :]], axis=0) / total
        q = exact(wq, tok, 0, 0)
        k = exact(wk, tok, 0, 0)
        v = exact(wv, tok, 0, 0)
        sc = exact(q, k, 0, 0) * scale
        e = jnp.where(same, jnp.exp(jnp.where(same, sc, 0.0)), 0.0)
        prob = e / jnp.sum(e, axis=1, keepdims=True)
        p_ref[b] = prob
        mix.append(exact(v, prob, 1, 1))
        kept.append((total, tok, q, k, v))
    hi, lo = split(spread_heads(jnp.concatenate(mix, axis=1)))
    bdm_ref[0] = hi
    bdm_ref[1] = lo

    sp = (dg(wb, bdm_ref[0], 1, 1) + dg(wb, bdm_ref[1], 1, 1)).astype(bf16)
    state = x_ref[...].astype(f32) + dg(sp, wout_ref[...], 1, 0)
    xhat2, rstd2 = norm_parts(state)
    normed2 = (xhat2 * gain2).astype(bf16)
    normed2t = normed2.T
    dy = dy_ref[...]
    for j in range(4):
        cols = slice(j * 256, (j + 1) * 256)
        u = dg(normed2, wup_ref[:, cols], 1, 0)
        u2 = u * u
        t = jnp.tanh(u * (GELU_C + (GELU_C * GELU_A) * u2))
        half = 0.5 + 0.5 * t
        hidden = (u * half).astype(bf16)
        slope = half + u * half * (1.0 - t) * (GELU_C + (3.0 * GELU_C * GELU_A) * u2)
        du = (dh_ref[:, cols].astype(f32) * slope).astype(bf16)
        du_ref[:, cols] = du
        g1[j * 256 : (j + 1) * 256, :] = dg(hidden, dy, 0, 0)
        g1[1024 + j * 256 : 1280 + j * 256, :] = dg(normed2t, du, 1, 0)
    dn = dg(du_ref[...], wup_ref[...], 1, 1).astype(bf16).astype(f32)
    g_gain2 = jnp.sum(dn * xhat2, axis=0, keepdims=True)
    ds = dy.astype(f32) + norm_back(dn, xhat2, rstd2, gain2)
    dstate_ref[...] = ds
    dsb = ds.astype(bf16)
    dsp = dg(dsb, wout_ref[...], 1, 1).astype(bf16)
    dmt = gather_heads(dg(dsp, wb, 0, 0))
    for j in range(8):
        s2[j] = dmt[(j % 2) * 16 : (j % 2 + 1) * 16, (j // 2) * 128 : (j // 2 + 1) * 128]
    sum2.step()
    big1.step()
    dw2_ref[...] = dg(dsp, bdm_ref[0], 1, 0) + dg(dsp, bdm_ref[1], 1, 0)
    sum2.step()
    big1.step()
    g2[0:256, :] = dg(sp, dsb, 0, 0)
    sum2.step()
    sum2.wait()

    gq = jnp.zeros((HEAD_DIM, HEAD_DIM), f32)
    gk, gv = gq, gq
    dwt, dtot = [], []
    for b in range(4):
        total, tok, q, k, v = kept[b]
        prob = p_ref[b]
        dm = jnp.concatenate([so2[2 * b], so2[2 * b + 1]], axis=0)
        dp = exact(dm, v, 0, 0)
        dsc = prob * (dp - jnp.sum(prob * dp, axis=1, keepdims=True)) * scale
        dq = exact(k, dsc, 1, 1)
        dk = exact(q, dsc, 1, 0)
        dv = exact(dm, prob, 1, 0)
        gq = gq + exact(tok, dq, 1, 1)
        gk = gk + exact(tok, dk, 1, 1)
        gv = gv + exact(tok, dv, 1, 1)
        dtok = exact(wq, dq, 1, 0) + exact(wk, dk, 1, 0) + exact(wv, dv, 1, 0)
        dtok = dtok / total
        dwt.append(dtok)
        dtot.append(-jnp.sum(dtok * tok, axis=0, keepdims=True))
    hi, lo = split(spread_heads(jnp.concatenate(dwt, axis=1)))
    bdw_ref[0] = hi
    bdw_ref[1] = lo
    d_totals = jnp.concatenate(dtot, axis=1)

    dfeat = (dg(wb, bdw_ref[0], 1, 1) + dg(wb, bdw_ref[1], 1, 1)).astype(bf16)
    g2[256:512, :] = dg(normed1t_ref[...], dfeat, 1, 0)
    mid2.step()
    dw = dw2_ref[...] + dg(feat, bdw_ref[0], 1, 0) + dg(feat, bdw_ref[1], 1, 0) + d_totals
    w = w_ref[...]
    dl = w * (dw - block_sum(w * dw, ones))
    dlt = (dl * inv_temp).astype(bf16)
    dmid = dg(dlt, bds_ref[...], 1, 1).astype(bf16)
    g3[0:256, :] = dg(normed1t_ref[...], dmid, 1, 0)
    big1.step()
    dn = dg(dmid, wmid_ref[...], 1, 1).astype(bf16).astype(f32) + dg(dfeat, wfeat_ref[...], 1, 1).astype(bf16).astype(
        f32
    )
    dn = dn.astype(bf16).astype(f32)
    xhat1, rstd1 = norm_parts(x_ref[...].astype(f32))

    first = (lax.axis_index("point") == 0).astype(f32)
    g3[SMALL:N3, :] = jnp.zeros((N3 - SMALL, 256), f32)
    pick = (iota((HM, 256), 0) // SLICES == iota((HM, 256), 1)).astype(f32)
    inv8 = jnp.zeros((1, 256), f32)
    for h in range(HEADS):
        inv8 = jnp.where(iota((1, 256), 1) == h, 1.0 / temp_ref[h], inv8)
    g_temp = jnp.sum(exact(fold8(dl * l_ref[...]), pick, 1, 0), axis=0, keepdims=True) * (-inv8)
    g3[SMALL : SMALL + 1, :] = jnp.sum(dn * xhat1, axis=0, keepdims=True)
    g3[SMALL + 1 : SMALL + 2, :] = g_gain2
    g3[SMALL + 2 : SMALL + 3, :] = g_temp
    g3[SMALL + 8 : SMALL + 40, 0:64] = exact(gather_heads(dg(midt_ref[...], dlt, 1, 0)), place, 1, 1)
    g3[SMALL + 8 : SMALL + 40, 128:160] = gq * first
    g3[SMALL + 40 : SMALL + 72, 0:32] = gk * first
    g3[SMALL + 40 : SMALL + 72, 128:160] = gv * first
    tail.step()
    mid2.step()
    big1.step()
    cells_ref[...] = (norm_back(dn, xhat1, rstd1, gain1) + dstate_ref[...]).astype(bf16)
    tail.step()
    big1.step()
    mid2.step()
    tail.step()
    big1.step()
    mid2.step()
    tail.step()
    big1.step()
    mid2.step()
    tail.step()
    big1.step()
    mid2.step()
    tail.step()
    mid2.step()
    big1.step()


def out_kernel(
    hbm_cells, hbm1, hbm2, hbm3,
    cells_out, gain1, mid, feat, slc, temp, wq, wk, wv, wout, gain2, up, down,
    o1, o3, sems,
):
    pairs = ((hbm1, o1), (hbm3, o3), (hbm_cells, cells_out), (hbm2.at[0:256, :], wout), (hbm2.at[256:512, :], feat))
    copies = [pltpu.make_async_copy(a, b, sems.at[i]) for i, (a, b) in enumerate(pairs)]
    for cp in copies:
        cp.start()
    copies[1].wait()
    mid[...] = o3[0:256, :]
    gain1[...] = o3[SMALL : SMALL + 1, :]
    gain2[...] = o3[SMALL + 1 : SMALL + 2, :]
    temp[...] = o3[SMALL + 2 : SMALL + 3, 0:8]
    slc[...] = o3[SMALL + 8 : SMALL + 40, 0:64]
    wq[...] = o3[SMALL + 8 : SMALL + 40, 128:160]
    wk[...] = o3[SMALL + 40 : SMALL + 72, 0:32]
    wv[...] = o3[SMALL + 40 : SMALL + 72, 128:160]
    copies[0].wait()
    down[...] = o1[0:1024, :]
    for j in range(4):
        up[:, j * 256 : (j + 1) * 256] = o1[1024 + j * 256 : 1280 + j * 256, :]
    for cp in copies[2:]:
        cp.wait()


vmem_ = pl.BlockSpec(memory_space=pltpu.VMEM)
any_ = pl.BlockSpec(memory_space=pl.ANY)


def vmem(count):
    return [vmem_] * count


def anys(count):
    return [any_] * count


def on_device(x, dy, gain1, wmid, wfeat, ws, temp, wq, wk, wv, wout, gain2, wup, wdown):
    sds = jax.ShapeDtypeStruct
    operands = (
        x[0], dy[0], gain1.reshape(1, D), wmid, wfeat, ws, wq, wk, wv, wout, gain2.reshape(1, D), wup, wdown,
    )
    cells, o1, o2, o3 = pl.pallas_call(
        main_kernel,
        out_shape=(sds((CELLS, D), bf16), sds((N1, 256), f32), sds((N2, 256), f32), sds((N3, 256), f32)),
        in_specs=[pl.BlockSpec(memory_space=pltpu.SMEM)] + [pl.BlockSpec(memory_space=pltpu.HBM)] * 13,
        out_specs=vmem(4),
        scratch_shapes=[pltpu.VMEM(a.shape, a.dtype) for a in operands]
        + [
            pltpu.SemaphoreType.DMA((13,)),
            pltpu.VMEM((CELLS, HM), f32),
            pltpu.VMEM((CELLS, HM), f32),
            pltpu.VMEM((CELLS, FF), bf16),
            pltpu.VMEM((CELLS, FF), bf16),
            pltpu.VMEM((D, CELLS), bf16),
            pltpu.VMEM((D, CELLS), bf16),
            pltpu.VMEM((CELLS, D), f32),
            pltpu.VMEM((CELLS, HM), f32),
            pltpu.VMEM((D, HM), bf16),
            pltpu.VMEM((2, D, HM), bf16),
            pltpu.VMEM((2, D, HM), bf16),
            pltpu.VMEM((4, 128, 128), f32),
        ]
        + small_scratch(24)
        + small_scratch(16)
        + big_scratch(N1)
        + mid_scratch(N2)
        + mid_scratch(N3),
        compiler_params=pltpu.CompilerParams(
            collective_id=0, has_side_effects=True, vmem_limit_bytes=56 * 2**20
        ),
    )(temp, *operands)
    outs = pl.pallas_call(
        out_kernel,
        out_shape=(
            sds((CELLS, D), bf16), sds((1, D), f32), sds((D, D), f32), sds((D, D), f32),
            sds((HEAD_DIM, SLICES), f32), sds((1, HEADS), f32), sds((HEAD_DIM, HEAD_DIM), f32),
            sds((HEAD_DIM, HEAD_DIM), f32), sds((HEAD_DIM, HEAD_DIM), f32), sds((D, D), f32), sds((1, D), f32),
            sds((D, FF), f32), sds((FF, D), f32),
        ),
        in_specs=[pl.BlockSpec(memory_space=pltpu.HBM)] * 4,
        out_specs=vmem(13),
        scratch_shapes=[
            pltpu.VMEM((N1, 256), f32),
            pltpu.VMEM((N3, 256), f32),
            pltpu.SemaphoreType.DMA((5,)),
        ],
        compiler_params=pltpu.CompilerParams(vmem_limit_bytes=56 * 2**20),
    )(cells, o1, o2, o3)
    outs = list(outs)
    outs[0] = outs[0][None]
    outs[1] = outs[1].reshape(D)
    outs[5] = outs[5].reshape(HEADS)
    outs[10] = outs[10].reshape(D)
    return tuple(outs)


def solution(mesh):
    return jax.shard_map(
        on_device,
        mesh=mesh,
        in_specs=(P("dp", "point", None), P("dp", "point", None)) + (P(),) * 12,
        out_specs=(P("dp", "point", None),) + (P(),) * 12,
        check_vma=False,
    )
```

time: 99.8 us -> 89.1 us (0.89)
  Pallas kernels: 95.1 us -> 88.2 us
  local copies, waits for them, and re-layouts: 3.8 us -> 0 us
    pallas_call x1, Pallas kernels: 93.2 us -> 84.5 us  [on_device(): pl.pallas_call(main_kernel, out_shape=(sds((CELLS, D), bf16), sds((N1, 25...]
    unnamed x6 -> x0, local copies, waits for them, and re-layouts: 3.8 us -> none
    pallas_call x1, Pallas kernels: 1.95 us -> 3.68 us  [on_device(): pl.pallas_call(out_kernel, out_shape=(sds((CELLS, D), bf16), sds((1, D),...]
where the time goes in v3:
time: 89.1 us; the launch traced here: 89 us
  Pallas kernels  88.2 us (99%)
    pallas_call x1, Pallas kernels, on_device(): pl.pallas_call(main_kernel, out_shape=(sds((CELLS, D), bf16), sds((N1, 25...  84.5 us
    pallas_call x1, Pallas kernels, on_device(): pl.pallas_call(out_kernel, out_shape=(sds((CELLS, D), bf16), sds((1, D),...  3.68 us

profile of v3, /device:TPU:1, one launch (start us, length us, event | category | flops | bytes accessed | tf_op | source)
XLA Modules:
  0.0 89.0 jit_solution(12642006801174141714)
XLA Ops:
  0.7 84.5 %shard_map.237 = (bf16[768,256]{1,0:T(8,128)(2,1)}, f32[2048,256]{1,0:T(8,128)}, f32[512,256]{1,0:T(8,128)}, f32[384,256]{1,0:T(8,128)}) custom-call(f32[8]{0:T(128)} %temp_ref.1, bf16[768,256]{1,0:T(8,128)(2,1)} %bitcast.8, bf16[768,256]{1,0:T(8,128)(2,1)} %bitcast.9, f32[1,256]{1,0:T(1,128)} %bitcast.10, bf16[256,256]{1,0:T(8,128)(2,1)} %rest_3_.1, ...), custom_call_target="tpu_custom_call" | custom-call | tf_op jit(solution)/shard_map/pallas_call | solution.py:606
  85.2 3.7 %shard_map.238 = (bf16[768,256]{1,0:T(8,128)(2,1)}, f32[1,256]{1,0:T(1,128)}, f32[256,256]{1,0:T(8,128)}, f32[256,256]{1,0:T(8,128)}, f32[32,64]{1,0:T(8,128)}, ...) custom-call(bf16[768,256]{1,0:T(8,128)(2,1)} %get-tuple-element.30.h, ...), custom_call_target="tpu_custom_call" | custom-call | tf_op jit(solution)/shard_map/pallas_call | solution.py:636

commit v4 on v3

--- a/solution.py
+++ b/solution.py
@@ -352,10 +352,12 @@
     temp_ref, *rest,
 ):
     hbm, outs, bufs, load_sem, rest = rest[:13], rest[13:17], rest[17:30], rest[30], rest[31:]
+    results, store_sem, rest = rest[:4], rest[4], rest[5:]
     x_ref, dy_ref, gain1_ref, wmid_ref, wfeat_ref, ws_ref, wq_ref, wk_ref, wv_ref, wout_ref, gain2_ref, wup_ref, wdown_ref = bufs
     (
     cells_ref, o1_ref, o2_ref, o3_ref,
-    ) = outs
+    ) = results
+    stores = [pltpu.make_async_copy(results[i], outs[i], store_sem.at[i]) for i in range(4)]
     (
     l_ref, w_ref, du_ref, dh_ref, normed1t_ref, midt_ref, dstate_ref, dw2_ref, bds_ref, bdm_ref, bdw_ref, p_ref,
     s1, so1, s1a, s1b, ss1, rs1, s2, so2, s2a, s2b, ss2, rs2,
@@ -449,7 +451,7 @@
     bdm_ref[0] = hi
     bdm_ref[1] = lo
 
-    sp = (dg(wb, bdm_ref[0], 1, 1) + dg(wb, bdm_ref[1], 1, 1)).astype(bf16)
+    sp = dg(wb, bdm_ref[0], 1, 1).astype(bf16)
     state = x_ref[...].astype(f32) + dg(sp, wout_ref[...], 1, 0)
     xhat2, rstd2 = norm_parts(state)
     normed2 = (xhat2 * gain2).astype(bf16)
@@ -485,6 +487,7 @@
     sum2.step()
     sum2.wait()
 
+    big1.step()
     gq = jnp.zeros((HEAD_DIM, HEAD_DIM), f32)
     gk, gv = gq, gq
     dwt, dtot = [], []
@@ -509,16 +512,16 @@
     bdw_ref[1] = lo
     d_totals = jnp.concatenate(dtot, axis=1)
 
-    dfeat = (dg(wb, bdw_ref[0], 1, 1) + dg(wb, bdw_ref[1], 1, 1)).astype(bf16)
+    dfeat = dg(wb, bdw_ref[0], 1, 1).astype(bf16)
     g2[256:512, :] = dg(normed1t_ref[...], dfeat, 1, 0)
     mid2.step()
     dw = dw2_ref[...] + dg(feat, bdw_ref[0], 1, 0) + dg(feat, bdw_ref[1], 1, 0) + d_totals
     w = w_ref[...]
     dl = w * (dw - block_sum(w * dw, ones))
     dlt = (dl * inv_temp).astype(bf16)
+    big1.step()
     dmid = dg(dlt, bds_ref[...], 1, 1).astype(bf16)
     g3[0:256, :] = dg(normed1t_ref[...], dmid, 1, 0)
-    big1.step()
     dn = dg(dmid, wmid_ref[...], 1, 1).astype(bf16).astype(f32) + dg(dfeat, wfeat_ref[...], 1, 1).astype(bf16).astype(
         f32
     )
@@ -543,6 +546,7 @@
     mid2.step()
     big1.step()
     cells_ref[...] = (norm_back(dn, xhat1, rstd1, gain1) + dstate_ref[...]).astype(bf16)
+    stores[0].start()
     tail.step()
     big1.step()
     mid2.step()
@@ -554,10 +558,13 @@
     mid2.step()
     tail.step()
     big1.step()
+    stores[1].start()
     mid2.step()
+    stores[2].start()
     tail.step()
-    mid2.step()
-    big1.step()
+    stores[3].start()
+    for cp in stores:
+        cp.wait()
 
 
 def out_kernel(
@@ -565,11 +572,13 @@
     cells_out, gain1, mid, feat, slc, temp, wq, wk, wv, wout, gain2, up, down,
     o1, o3, sems,
 ):
-    pairs = ((hbm1, o1), (hbm3, o3), (hbm_cells, cells_out), (hbm2.at[0:256, :], wout), (hbm2.at[256:512, :], feat))
+    part = N1 // 8
+    pairs = [(hbm3, o3), (hbm_cells, cells_out), (hbm2.at[0:256, :], wout), (hbm2.at[256:512, :], feat)]
+    pairs += [(hbm1.at[k * part : (k + 1) * part, :], o1.at[k * part : (k + 1) * part, :]) for k in range(8)]
     copies = [pltpu.make_async_copy(a, b, sems.at[i]) for i, (a, b) in enumerate(pairs)]
     for cp in copies:
         cp.start()
-    copies[1].wait()
+    copies[0].wait()
     mid[...] = o3[0:256, :]
     gain1[...] = o3[SMALL : SMALL + 1, :]
     gain2[...] = o3[SMALL + 1 : SMALL + 2, :]
@@ -578,11 +587,13 @@
     wq[...] = o3[SMALL + 8 : SMALL + 40, 128:160]
     wk[...] = o3[SMALL + 40 : SMALL + 72, 0:32]
     wv[...] = o3[SMALL + 40 : SMALL + 72, 128:160]
-    copies[0].wait()
-    down[...] = o1[0:1024, :]
     for j in range(4):
+        copies[4 + j].wait()
+        down[j * 256 : (j + 1) * 256, :] = o1[j * 256 : (j + 1) * 256, :]
+    for j in range(4):
+        copies[8 + j].wait()
         up[:, j * 256 : (j + 1) * 256] = o1[1024 + j * 256 : 1280 + j * 256, :]
-    for cp in copies[2:]:
+    for cp in copies[1:4]:
         cp.wait()
 
 
@@ -607,10 +618,15 @@
         main_kernel,
         out_shape=(sds((CELLS, D), bf16), sds((N1, 256), f32), sds((N2, 256), f32), sds((N3, 256), f32)),
         in_specs=[pl.BlockSpec(memory_space=pltpu.SMEM)] + [pl.BlockSpec(memory_space=pltpu.HBM)] * 13,
-        out_specs=vmem(4),
+        out_specs=[pl.BlockSpec(memory_space=pltpu.HBM)] * 4,
         scratch_shapes=[pltpu.VMEM(a.shape, a.dtype) for a in operands]
         + [
             pltpu.SemaphoreType.DMA((13,)),
+            pltpu.VMEM((CELLS, D), bf16),
+            pltpu.VMEM((N1, 256), f32),
+            pltpu.VMEM((N2, 256), f32),
+            pltpu.VMEM((N3, 256), f32),
+            pltpu.SemaphoreType.DMA((4,)),
             pltpu.VMEM((CELLS, HM), f32),
             pltpu.VMEM((CELLS, HM), f32),
             pltpu.VMEM((CELLS, FF), bf16),
@@ -646,7 +662,7 @@
         scratch_shapes=[
             pltpu.VMEM((N1, 256), f32),
             pltpu.VMEM((N3, 256), f32),
-            pltpu.SemaphoreType.DMA((5,)),
+            pltpu.SemaphoreType.DMA((12,)),
         ],
         compiler_params=pltpu.CompilerParams(vmem_limit_bytes=56 * 2**20),
     )(cells, o1, o2, o3)

time: 89.1 us -> 83.3 us (0.935)
  Pallas kernels: 88.2 us -> 82.4 us
    pallas_call x1, Pallas kernels: 84.5 us -> 78.6 us  [on_device(): pl.pallas_call(main_kernel, out_shape=(sds((CELLS, D), bf16), sds((N1, 25...]
where the time goes in v4:
time: 83.3 us; the launch traced here: 83.2 us
  Pallas kernels  82.4 us (99%)
    pallas_call x1, Pallas kernels, on_device(): pl.pallas_call(main_kernel, out_shape=(sds((CELLS, D), bf16), sds((N1, 25...  78.6 us
    pallas_call x1, Pallas kernels, on_device(): pl.pallas_call(out_kernel, out_shape=(sds((CELLS, D), bf16), sds((1, D),...  3.77 us

profile of v4, /device:TPU:1, one launch (start us, length us, event | category | flops | bytes accessed | tf_op | source)
XLA Modules:
  0.0 83.2 jit_solution(18133376077461773759)
XLA Ops:
  0.7 78.6 %shard_map.237 = (bf16[768,256]{1,0:T(8,128)(2,1)}, f32[2048,256]{1,0:T(8,128)}, f32[512,256]{1,0:T(8,128)}, f32[384,256]{1,0:T(8,128)}) custom-call(f32[8]{0:T(128)} %temp_ref.1, bf16[768,256]{1,0:T(8,128)(2,1)} %bitcast.8, bf16[768,256]{1,0:T(8,128)(2,1)} %bitcast.9, f32[1,256]{1,0:T(1,128)} %bitcast.10, bf16[256,256]{1,0:T(8,128)(2,1)} %rest_3_.1, ...), custom_call_target="tpu_custom_call" | custom-call | tf_op jit(solution)/shard_map/pallas_call | solution.py:617
  79.3 3.8 %shard_map.238 = (bf16[768,256]{1,0:T(8,128)(2,1)}, f32[1,256]{1,0:T(1,128)}, f32[256,256]{1,0:T(8,128)}, f32[256,256]{1,0:T(8,128)}, f32[32,64]{1,0:T(8,128)}, ...) custom-call(bf16[768,256]{1,0:T(8,128)(2,1)} %get-tuple-element.30.h, ...), custom_call_target="tpu_custom_call" | custom-call | tf_op jit(solution)/shard_map/pallas_call | solution.py:652

commit v5 on v4

--- a/solution.py
+++ b/solution.py
@@ -545,9 +545,9 @@
     tail.step()
     mid2.step()
     big1.step()
+    tail.step()
     cells_ref[...] = (norm_back(dn, xhat1, rstd1, gain1) + dstate_ref[...]).astype(bf16)
     stores[0].start()
-    tail.step()
     big1.step()
     mid2.step()
     tail.step()

time: 83.3 us -> 83.3 us (level)
  no operation moved by 1% of the time
where the time goes in v5:
time: 83.3 us; the launch traced here: 83.1 us
  Pallas kernels  82.3 us (99%)
    pallas_call x1, Pallas kernels, on_device(): pl.pallas_call(main_kernel, out_shape=(sds((CELLS, D), bf16), sds((N1, 25...  78.6 us
    pallas_call x1, Pallas kernels, on_device(): pl.pallas_call(out_kernel, out_shape=(sds((CELLS, D), bf16), sds((1, D),...  3.77 us

profile of v5, /device:TPU:1, one launch (start us, length us, event | category | flops | bytes accessed | tf_op | source)
XLA Modules:
  0.0 83.1 jit_solution(12288279878465026155)
XLA Ops:
  0.7 78.6 %shard_map.237 = (bf16[768,256]{1,0:T(8,128)(2,1)}, f32[2048,256]{1,0:T(8,128)}, f32[512,256]{1,0:T(8,128)}, f32[384,256]{1,0:T(8,128)}) custom-call(f32[8]{0:T(128)} %temp_ref.1, bf16[768,256]{1,0:T(8,128)(2,1)} %bitcast.8, bf16[768,256]{1,0:T(8,128)(2,1)} %bitcast.9, f32[1,256]{1,0:T(1,128)} %bitcast.10, bf16[256,256]{1,0:T(8,128)(2,1)} %rest_3_.1, ...), custom_call_target="tpu_custom_call" | custom-call | tf_op jit(solution)/shard_map/pallas_call | solution.py:617
  79.2 3.8 %shard_map.238 = (bf16[768,256]{1,0:T(8,128)(2,1)}, f32[1,256]{1,0:T(1,128)}, f32[256,256]{1,0:T(8,128)}, f32[256,256]{1,0:T(8,128)}, f32[32,64]{1,0:T(8,128)}, ...) custom-call(bf16[768,256]{1,0:T(8,128)(2,1)} %get-tuple-element.30.h, ...), custom_call_target="tpu_custom_call" | custom-call | tf_op jit(solution)/shard_map/pallas_call | solution.py:652
